TPU v7x, 256 devices: a whole 4x4x8 slice. The times are simulated.
256 devices in a mesh: kz: 8 (over x, core), tile: 32 (over y, z).
Axes of the slice: x: 4, y: 4, z: 8, core: 2. Of those that a mesh axis runs over, the one named last changes fastest.
Arguments:
- coil_data: bfloat16 [8, 32, 8, 32, 2, 16, 128], P('kz', 'tile'), may hold values from -6 to 6
- frame_of: int32 [8, 32, 8, 32, 2], P('kz', 'tile'), may hold values from 0 to 999
- basis: bfloat16 [1000, 10], replicated, may hold values from -4 to 4
- sample_pos: float32 [8, 32, 8, 32, 2, 2, 128], P('kz', 'tile'), may hold values from 1.5 to 30.5, as said below
- window_at: int32 [8, 32, 8, 32, 2, 2], P('kz', 'tile'), may hold values from -2 to 639, as said below
- live_count: int32 [8, 32, 8, 32], P('kz', 'tile'), may hold values from 0 to 2, as said below
Outputs:
- image: bfloat16 [8, 640, 102400], P('kz', None, 'tile')
Inputs may be any that keep to these rules, and one draw needn't show every extreme that they name: `live_count`: live slots of a pair are its first ones; destination tiles from 12 up to but not including 32 * 5 // 8 receive every slot from every acquiring device. `window_at`: the first entry (row0) lies in -2 to 18, the second (col0) in 0 to 639. `sample_pos`: the first entry lies in 1.5 to 2.5, the second in 1.5 to 32 - 1.5.
All inputs are finite; a program needn't handle non-finite values.
Results may differ from a plain program's by a relative error of at most 0.0077.
Values may be sent and summed in bfloat16 or wider, within the bound.
A program may use at most 192 MiB of HBM per device.

v0:
```python
import math

import jax
import jax.numpy as jnp
from jax import lax
from jax.sharding import PartitionSpec as P

PLANE = 640
WIN_ROWS = 4
WIN_COLS = 32


def cut_along(shard, dim, length):
    before, after = (shard.shape[:dim], shard.shape[dim + 1 :])
    return jnp.moveaxis(shard.reshape(*before, length, -1, *after), dim, 0)


def in_order(blocks, dim):
    blocks = jnp.moveaxis(blocks, 0, dim)
    lengths = blocks.shape
    return blocks.reshape(*lengths[:dim], lengths[dim] * lengths[dim + 1], *lengths[dim + 2 :])


def exchange_both(shard, axis, axes, splits, concats):
    sizes = [lax.axis_size(a) for a in axes]
    blocks = cut_along(shard, splits[0], sizes[0])
    blocks = jnp.moveaxis(cut_along(blocks, splits[1] + 1, sizes[1]), 0, 1)
    inside = blocks.shape[2:]
    blocks = blocks.reshape(-1, *inside)
    blocks = lax.all_to_all(blocks, axis, split_axis=0, concat_axis=0, tiled=True)
    blocks = in_order(blocks.reshape(*sizes, *inside), concats[0] + 1)
    return in_order(blocks, concats[1])


def from_behind(value, axis, steps):
    count = lax.axis_size(axis)
    pairs = [(source, (source + steps) % count) for source in range(count)]
    return lax.ppermute(value, axis, pairs)


def taper(dist):
    inner = 1.0 - (dist / 1.5) ** 2
    return jnp.maximum(inner, 0.0) ** 2


def project(blocks, coeffs):
    count = blocks.shape[0]
    coils = blocks.shape[1] // 2
    ranks = coeffs.shape[1]
    samples = blocks.shape[2]
    data = blocks.astype(jnp.float32).reshape(count, 2, 1, coils, samples)
    scale = coeffs.astype(jnp.float32).reshape(count, 1, ranks, 1, 1)
    return (data * scale).reshape(count, 2 * ranks * coils, samples).astype(jnp.bfloat16)


def grid_tile(proj, offsets, corners, alive, tile_rows, plane):
    count, width, samples = proj.shape
    group = 64
    row_cells = jnp.arange(WIN_ROWS, dtype=jnp.float32)
    col_cells = jnp.arange(WIN_COLS, dtype=jnp.float32)
    cells = jnp.arange(WIN_ROWS * WIN_COLS, dtype=jnp.int32)
    cell_row = cells // WIN_COLS
    cell_col = cells % WIN_COLS

    def step(acc, items):
        values, place, corner, living = items
        row_k = taper(row_cells[None, :, None] - place[:, 0:1, :])
        col_k = taper(col_cells[None, :, None] - place[:, 1:2, :])
        weights = (row_k[:, :, None, :] * col_k[:, None, :, :]).reshape(
            group, WIN_ROWS * WIN_COLS, samples
        )
        weights = (weights * living[:, None, None]).astype(jnp.bfloat16)
        contrib = jnp.einsum("gwb,gcb->gwc", weights, values, preferred_element_type=jnp.float32)
        rows = corner[:, 0:1] + 2 + cell_row[None, :]
        cols = (corner[:, 1:2] + cell_col[None, :]) % plane
        acc = acc.at[rows.reshape(-1), cols.reshape(-1)].add(contrib.reshape(-1, width))
        return (acc, None)

    start = jnp.zeros((tile_rows + 4, plane, width), jnp.float32)
    items = (
        proj.reshape(-1, group, width, samples),
        offsets.reshape(-1, group, 2, samples),
        corners.reshape(-1, group, 2),
        alive.reshape(-1, group),
    )
    acc, _ = lax.scan(step, start, items)
    return acc


def tables(n):
    idx = jnp.arange(n, dtype=jnp.int32)
    phase = (idx[:, None] * idx[None, :] % n).astype(jnp.float32) * (2.0 * math.pi / n)
    return (jnp.cos(phase).astype(jnp.bfloat16), jnp.sin(phase).astype(jnp.bfloat16))


def combine(first, second, half):
    return jnp.concatenate(
        [first[..., :half] - second[..., half:], second[..., :half] + first[..., half:]], axis=-1
    )


def body(coil_data, frame_of, basis, sample_pos, window_at, live_count):
    parts = coil_data.shape[2]
    tiles = coil_data.shape[3]
    slots = coil_data.shape[4]
    pair = coil_data.shape[5]
    samples = coil_data.shape[6]
    width = 2 * basis.shape[1] * (pair // 2)
    half = width // 2
    tile_rows = PLANE // tiles
    raw = exchange_both(coil_data, ("kz", "tile"), ("kz", "tile"), (2, 3), (0, 1))
    frames = exchange_both(frame_of, ("kz", "tile"), ("kz", "tile"), (2, 3), (0, 1))
    arrived = project(raw.reshape(-1, pair, samples), basis[frames.reshape(-1)])
    slot_idx = jnp.arange(slots, dtype=jnp.int32)
    counts = live_count.reshape(parts, tiles)
    alive = (slot_idx[None, None, :] < counts[:, :, None]).astype(jnp.float32)
    acc = grid_tile(
        arrived,
        sample_pos.reshape(-1, 2, samples),
        window_at.reshape(-1, 2),
        alive.reshape(-1),
        tile_rows,
        PLANE,
    )
    from_above = from_behind(acc[tile_rows + 2 : tile_rows + 4], "tile", 1)
    from_below = from_behind(acc[0:2], "tile", -1)
    core = acc[2 : tile_rows + 2]
    core = core.at[0:2].add(from_above)
    core = core.at[tile_rows - 2 : tile_rows].add(from_below)
    grid = core.astype(jnp.bfloat16)
    cos_tab, sin_tab = tables(PLANE)
    first = jnp.einsum("xkq,ky->xyq", grid, cos_tab, preferred_element_type=jnp.float32)
    second = jnp.einsum("xkq,ky->xyq", grid, sin_tab, preferred_element_type=jnp.float32)
    mid = combine(first, second, half).astype(jnp.bfloat16)
    columns = lax.all_to_all(mid, "tile", split_axis=1, concat_axis=0, tiled=True)
    first = jnp.einsum("kyq,kx->xyq", columns, cos_tab, preferred_element_type=jnp.float32)
    second = jnp.einsum("kyq,kx->xyq", columns, sin_tab, preferred_element_type=jnp.float32)
    result = (combine(first, second, half) * (1.0 / PLANE)).astype(jnp.bfloat16)
    return result.reshape(1, result.shape[0], -1)


def solution(mesh):
    return jax.shard_map(
        body,
        mesh=mesh,
        in_specs=(
            P("kz", "tile", None, None, None, None, None),
            P("kz", "tile", None, None, None),
            P(),
            P("kz", "tile", None, None, None, None, None),
            P("kz", "tile", None, None, None, None),
            P("kz", "tile", None, None),
        ),
        out_specs=P("kz", None, "tile"),
        check_vma=False,
    )
```

profile of v0, /device:TPU:32, one launch (start us, length us, event | category | flops | bytes accessed | tf_op | source)
XLA Modules:
  0.0 984.5 jit_solution(7586445230939341597)
XLA Ops:
  0.9 26.7 %all_to_all.28 = s32[256,1,1,1,1,2]{5,4,3,2,1,0:T(1,128)S(1)} all-to-all(s32[256,1,1,1,1,2]{5,4,3,2,1,0:T(1,128)S(1)} %bitcast.134), channel_id=1, replica_groups=mesh['kz'=8,'tile'=32] {'kz','tile'}, dimensions={0} | all-to-all | bytes 4096 | tf_op jit(solution)/shard_map/all_to_all | solution.py:30
  37.9 49.1 %all-to-all-done = bf16[256,1,1,1,1,2,16,128]{7,6,5,4,3,2,1,0:T(8,128)(2,1)S(1)} async-done(((bf16[256,1,1,1,1,2,16,128]{7,6,5,4,3,2,1,0:T(8,128)(2,1)}), bf16[256,1,1,1,1,2,16,128]{7,6,5,4,3,2,1,0:T(8,128)(2,1)S(1)}, u32[]{:S(2)}, u32[]{:S(2)}) %all-to-all-start) | async-done | bytes 2097184 | tf_op jit(solution)/shard_map/all_to_all | solution.py:30
  87.0 13.5 %mul.124 = f32[512,2,10,8,128]{4,3,2,1,0:T(8,128)} broadcast(bf16[512,2,8,128]{3,2,1,0:T(8,128)(2,1)S(1)} %bitcast.120), dimensions={0,1,3,4} | broadcast | bytes 44040192 | tf_op jit(solution)/shard_map/mul | solution.py:53
  100.6 21.5 %multiply_convert_fusion = bf16[8,64,160,128]{3,2,1,0:T(8,128)(2,1)} fusion(f32[8,64,160,128]{3,2,1,0:T(8,128)} %bitcast.117, f32[8,64,160]{2,1,0:T(8,128)S(1)} %copy.82), kind=kLoop, calls=%fused_computation.47 | loop fusion | flops 20971520 | bytes 63242240 | tf_op jit(solution)/shard_map/convert_element_type | solution.py:53
  122.0 7.3 broadcast_in_dim.2
  129.3 520.4 %while.15 = (s32[]{:T(128)}, f32[24,640,160]{2,1,0:T(8,128)}, s32[8,64,2]{1,2,0:T(2,128)S(1)}, f32[8,64,2,128]{3,1,2,0:T(8,128)}, f32[8,64]{1,0:T(8,128)S(1)}, /...) while((s32[]{:T(128)}, f32[24,640,160]{2,1,0:T(8,128)}, ...), condition=%wide.region_2.3_spmd.clone, body=%wide.region_0.2_spmd.clone.sunk | while | flops 342009408 | bytes 39343992 | solution.py:86
  138.8 55.5 %scatter_fusion = f32[15360,160]{1,0:T(8,128)} fusion(f32[15360,160]{1,0:T(8,128)} %bitcast.114, s32[8192]{0:T(1024)S(1)} %broadcast_select_fusion.2, f32[8192,160]{1,0:T(8,128)} %bitcast.116), kind=kCustom, calls=%fused_computation.1.clone.clone.1 | custom fusion | flops 1310720 | bytes 15761408 | tf_op jit(solution)/shard_map/while
  203.9 55.5 %scatter_fusion = f32[15360,160]{1,0:T(8,128)} fusion(f32[15360,160]{1,0:T(8,128)} %bitcast.114, s32[8192]{0:T(1024)S(1)} %broadcast_select_fusion.2, f32[8192,160]{1,0:T(8,128)} %bitcast.116), kind=kCustom, calls=%fused_computation.1.clone.clone.1 | custom fusion | flops 1310720 | bytes 15761408 | tf_op jit(solution)/shard_map/while
  262.2 6.7 fusion.69
  269.0 55.5 %scatter_fusion = f32[15360,160]{1,0:T(8,128)} fusion(f32[15360,160]{1,0:T(8,128)} %bitcast.114, s32[8192]{0:T(1024)S(1)} %broadcast_select_fusion.2, f32[8192,160]{1,0:T(8,128)} %bitcast.116), kind=kCustom, calls=%fused_computation.1.clone.clone.1 | custom fusion | flops 1310720 | bytes 15761408 | tf_op jit(solution)/shard_map/while
  327.3 6.7 fusion.69
  334.0 55.5 %scatter_fusion = f32[15360,160]{1,0:T(8,128)} fusion(f32[15360,160]{1,0:T(8,128)} %bitcast.114, s32[8192]{0:T(1024)S(1)} %broadcast_select_fusion.2, f32[8192,160]{1,0:T(8,128)} %bitcast.116), kind=kCustom, calls=%fused_computation.1.clone.clone.1 | custom fusion | flops 1310720 | bytes 15761408 | tf_op jit(solution)/shard_map/while
  392.3 6.7 fusion.69
  399.1 55.5 %scatter_fusion = f32[15360,160]{1,0:T(8,128)} fusion(f32[15360,160]{1,0:T(8,128)} %bitcast.114, s32[8192]{0:T(1024)S(1)} %broadcast_select_fusion.2, f32[8192,160]{1,0:T(8,128)} %bitcast.116), kind=kCustom, calls=%fused_computation.1.clone.clone.1 | custom fusion | flops 1310720 | bytes 15761408 | tf_op jit(solution)/shard_map/while
  457.4 6.7 fusion.69
  464.1 55.5 %scatter_fusion = f32[15360,160]{1,0:T(8,128)} fusion(f32[15360,160]{1,0:T(8,128)} %bitcast.114, s32[8192]{0:T(1024)S(1)} %broadcast_select_fusion.2, f32[8192,160]{1,0:T(8,128)} %bitcast.116), kind=kCustom, calls=%fused_computation.1.clone.clone.1 | custom fusion | flops 1310720 | bytes 15761408 | tf_op jit(solution)/shard_map/while
  522.4 6.7 fusion.69
  529.2 55.5 %scatter_fusion = f32[15360,160]{1,0:T(8,128)} fusion(f32[15360,160]{1,0:T(8,128)} %bitcast.114, s32[8192]{0:T(1024)S(1)} %broadcast_select_fusion.2, f32[8192,160]{1,0:T(8,128)} %bitcast.116), kind=kCustom, calls=%fused_computation.1.clone.clone.1 | custom fusion | flops 1310720 | bytes 15761408 | tf_op jit(solution)/shard_map/while
  587.5 6.7 fusion.69
  594.2 55.5 %scatter_fusion = f32[15360,160]{1,0:T(8,128)} fusion(f32[15360,160]{1,0:T(8,128)} %bitcast.114, s32[8192]{0:T(1024)S(1)} %broadcast_select_fusion.2, f32[8192,160]{1,0:T(8,128)} %bitcast.116), kind=kCustom, calls=%fused_computation.1.clone.clone.1 | custom fusion | flops 1310720 | bytes 15761408 | tf_op jit(solution)/shard_map/while
  649.7 13.9 %copy.85 = f32[24,640,160]{1,2,0:T(8,128)} copy(f32[24,640,160]{2,1,0:T(8,128)} %get-tuple-element.155) | data formatting | bytes 19660800 | tf_op jit(solution)/shard_map/while | solution.py:86
  667.4 18.8 %collective-permute-done = f32[2,640,160]{1,2,0:T(8,128)S(1)} collective-permute-done((f32[2,640,160]{1,2,0:T(8,128)S(1)}, f32[2,640,160]{1,2,0:T(8,128)S(1)}, u32[]{:S(2)}, u32[]{:S(2)}) %collective-permute-start) | collective-permute-done | bytes 819232 | tf_op jit(solution)/shard_map/ppermute | solution.py:38
  687.0 12.5 %fusion.34 = f32[640,3200]{0,1} fusion(bf16[640,3200]{0,1:T(8,128)(2,1)S(1)} %bitcast.125), kind=kOutput, calls=%fused_computation.70 | convolution fusion | flops 2625536000 | bytes 12288000
  699.6 12.5 %fusion.36 = f32[640,3200]{0,1} fusion(bf16[640,3200]{0,1:T(8,128)(2,1)S(1)} %bitcast.126), kind=kOutput, calls=%fused_computation.72 | convolution fusion | flops 2625536000 | bytes 12288000
  712.1 6.8 fusion.26
  721.2 10.9 %copy.89 = bf16[20,640,160]{2,0,1:T(8,128)(2,1)} copy(bf16[20,640,160]{1,2,0:T(8,128)(2,1)} %pad_maximum_fusion) | data formatting | bytes 8192000 | tf_op jit(solution)/shard_map/concatenate | solution.py:97
  732.1 185.1 %all_to_all.29 = bf16[20,640,160]{2,0,1:T(8,128)(2,1)S(1)} all-to-all(bf16[20,640,160]{2,0,1:T(8,128)(2,1)} %copy.89), channel_id=1, replica_groups=mesh['kz'=8,'tile'=32] {'tile'}, dimensions={1} | all-to-all | bytes 8192000 | tf_op jit(solution)/shard_map/all_to_all | solution.py:135
  921.1 11.7 %all_to_all.24 = bf16[640,20,160]{2,0,1:T(8,128)(2,1)} reshape(bf16[32,20,20,160]{3,1,0,2:T(8,128)(2,1)} %copy.91) | data formatting | bytes 8192000 | tf_op jit(solution)/shard_map/all_to_all | solution.py:135
  932.8 8.7 copy.92
  941.6 14.7 %fusion.35 = f32[640,3200]{0,1} fusion(bf16[640,3200]{0,1:T(8,128)(2,1)} %bitcast.127), kind=kOutput, calls=%fused_computation.71 | convolution fusion | flops 2625536000 | bytes 12288000
  956.2 12.5 %fusion.37 = f32[640,3200]{0,1} fusion(bf16[640,3200]{0,1:T(8,128)(2,1)S(1)} %bitcast.128), kind=kOutput, calls=%fused_computation.73 | convolution fusion | flops 2625536000 | bytes 12288000
  977.7 6.8 copy.94
  (187 shorter events, 66.4 us)
Async XLA Ops:
  0.0 33.9 %copy-start.3 = (bf16[1000,10]{0,1:T(8,128)(2,1)S(1)}, bf16[1000,10]{0,1:T(8,128)(2,1)}, u32[]{:S(2)}) copy-start(bf16[1000,10]{0,1:T(8,128)(2,1)} %param.14) | copy-start | bytes 60004
  0.0 34.1 %copy-start.2 = (f32[1,1,8,32,2,2,128]{6,5,4,3,2,1,0:T(2,128)S(1)}, f32[1,1,8,32,2,2,128]{6,5,4,3,2,1,0:T(2,128)}, u32[]{:S(2)}) copy-start(f32[1,1,8,32,2,2,128]{6,5,4,3,2,1,0:T(2,128)} %param.15) | copy-start | bytes 1572868
  0.0 35.2 %copy-start.7 = (s32[1,1,8,32]{3,2,1,0:T(8,128)S(1)}, s32[1,1,8,32]{3,2,1,0:T(8,128)}, u32[]{:S(2)}) copy-start(s32[1,1,8,32]{3,2,1,0:T(8,128)} %param.17) | copy-start | bytes 3076
  0.0 35.5 %copy-start.4 = (s32[1,1,8,32,2,2]{3,5,4,2,1,0:T(2,128)S(1)}, s32[1,1,8,32,2,2]{3,5,4,2,1,0:T(2,128)}, u32[]{:S(2)}) copy-start(s32[1,1,8,32,2,2]{3,5,4,2,1,0:T(2,128)} %param.16) | copy-start | bytes 12292
  27.6 59.4 %all-to-all-start = ((bf16[256,1,1,1,1,2,16,128]{7,6,5,4,3,2,1,0:T(8,128)(2,1)}), bf16[256,1,1,1,1,2,16,128]{7,6,5,4,3,2,1,0:T(8,128)(2,1)S(1)}, u32[]{:S(2)}, u32[]{:S(2)}) async-start(bf16[256,1,1,1,1,2,16,128]{7,6,5,4,3,2,1,0:T(8,128)(2,1)} %bitcast.131), calls=%async_computation | async-start | bytes 4194304 | tf_op jit(solution)/shard_map/all_to_all | solution.py:30
  122.0 7.3 copy-start.5
  122.0 7.3 copy-start.6
  663.6 22.5 %copy-start = (f32[24,640,160]{1,2,0:T(8,128)S(1)}, f32[24,640,160]{1,2,0:T(8,128)}, u32[]{:S(2)}) copy-start(f32[24,640,160]{1,2,0:T(8,128)} %copy.85) | copy-start | bytes 29491204
  665.2 20.9 %collective-permute-start = (f32[2,640,160]{1,2,0:T(8,128)S(1)}, f32[2,640,160]{1,2,0:T(8,128)S(1)}, u32[]{:S(2)}, u32[]{:S(2)}) collective-permute-start(f32[2,640,160]{1,2,0:T(8,128)S(1)} %get-tuple-element.220), channel_id=1, source_target_pairs={{0,1},{1,2},{2,3},{3,4},{4,5},{5,6},{6,7},{7,8},{8,9},{9,10},{10,1... | collective-permute-start | bytes 2457608 | tf_op jit(solution)/shard_map/ppermute | solution.py:38
  665.7 20.4 %slice-start = ((f32[24,640,160]{1,2,0:T(8,128)}), f32[20,640,160]{1,2,0:T(8,128)S(1)}, s32[]{:S(2)}) async-start(f32[24,640,160]{1,2,0:T(8,128)} %copy.85), calls=%async_computation.3 | async-start | bytes 16384000 | tf_op jit(solution)/shard_map/slice | solution.py:127
  665.7 20.7 %collective-permute-start.1 = (f32[2,640,160]{1,2,0:T(8,128)S(1)}, f32[2,640,160]{1,2,0:T(8,128)S(1)}, u32[]{:S(2)}, u32[]{:S(2)}) collective-permute-start(f32[2,640,160]{1,2,0:T(8,128)S(1)} %get-tuple-element.219), channel_id=1, source_target_pairs={{0,31},{1,0},{2,1},{3,2},{4,3},{5,4},{6,5},{7,6},{8,7},{9,8},{10,9... | collective-permute-start | bytes 2457608 | tf_op jit(solution)/shard_map/ppermute | solution.py:38
  941.6 14.7 %copy-start.1 = (bf16[640,20,160]{0,2,1:T(8,128)(2,1)S(1)}, bf16[640,20,160]{0,2,1:T(8,128)(2,1)}, u32[]{:S(2)}) copy-start(bf16[640,20,160]{0,2,1:T(8,128)(2,1)} %copy.92) | copy-start | bytes 12288004
where the time goes:
time: 987 us; the launch traced here: 985 us
  other arithmetic  499 us (51%)
  blocking collectives  212 us (21%)
  matrix products  106 us (11%)
  local copies, waits for them, and re-layouts  90.2 us (9%)
  waiting for transfers between devices  68.1 us (7%)
    while x32, other arithmetic  447 us
    all_to_all x1, blocking collectives, body(): lax.all_to_all(mid, 'tile', split_axis=1, concat_axis=0, tiled=True)  185 us
    reshape x8, matrix products, step(): contrib.reshape(-1, width)  53.7 us
    unnamed x4, matrix products  52.2 us
    all_to_all x1, waiting for transfers between devices, exchange_both(): lax.all_to_all(blocks, axis, split_axis=0, concat_axis=0, tiled=True)  49.1 us
    all_to_all x1, blocking collectives, exchange_both(): lax.all_to_all(blocks, axis, split_axis=0, concat_axis=0, tiled=True)  26.7 us
    all_to_all x3, local copies, waits for them, and re-layouts, body(): lax.all_to_all(mid, 'tile', split_axis=1, concat_axis=0, tiled=True)  24.4 us
    convert_element_type x1, other arithmetic, project(): (data * scale).reshape(count, 2 * ranks * coils, samples)  21.5 us
  transfers between devices with their start and end apart: 3, of which 3 were waited for; matrix products, arithmetic and copies ran while one was open for 0% of the time, Pallas kernels for 0%

commit v1 on v0

v1 whole, which is shorter than its diff:
```python
import functools
import math

import jax
import jax.numpy as jnp
from jax import lax
from jax.experimental import pallas as pl
from jax.experimental.pallas import tpu as pltpu
from jax.sharding import PartitionSpec as P

PLANE = 640
WIN_ROWS = 4
WIN_COLS = 32
TILE_ROWS = 20
WIDE = 40
PAD = 680
LANES = 128
HALF = 80
MB = 1024 * 1024


def taper(dist):
    inner = 1.0 - (dist * (1.0 / 1.5)) * (dist * (1.0 / 1.5))
    inner = jnp.maximum(inner, 0.0)
    return inner * inner


def grid_slots(row_ref, col_ref, live_ref, coef_ref, pos_ref, data_ref, acc_ref, batch):
    count = data_ref.shape[0]
    row_cell = lax.broadcasted_iota(jnp.int32, (8, LANES), 0)
    col_cell = lax.broadcasted_iota(jnp.int32, (WIDE, LANES), 0)
    zero = jnp.zeros((LANES - HALF, LANES), jnp.bfloat16)

    def contribution(s):
        col0 = col_ref[s]
        shift = jnp.bitwise_and(col0, 7)
        place = pos_ref[s]
        u = place[0:1, :]
        v = place[1:2, :]
        row_k = taper(row_cell.astype(jnp.float32) - u) * live_ref[s]
        col_k = taper((col_cell - shift).astype(jnp.float32) - v)
        weight = jnp.concatenate([row_k[i : i + 1, :] * col_k for i in range(WIN_ROWS)], axis=0)
        weight = weight.astype(jnp.bfloat16)
        data = data_ref[s].astype(jnp.float32)
        re, im = data[0:8], data[8:16]
        scale = [coef_ref[s * 10 + r] for r in range(10)]
        re = jnp.concatenate([re * c for c in scale], axis=0).astype(jnp.bfloat16)
        im = jnp.concatenate([im * c for c in scale], axis=0).astype(jnp.bfloat16)
        values = jnp.concatenate([re, zero, im, zero], axis=0)
        return lax.dot_general(
            weight, values, (((1,), (1,)), ((), ())), preferred_element_type=jnp.float32
        )

    def step(b, carry):
        slots = [b * batch + k for k in range(batch)]
        parts = [contribution(s) for s in slots]
        for s, part in zip(slots, parts):
            row = row_ref[s] + 2
            start = pl.multiple_of(jnp.bitwise_and(col_ref[s], -8), 8)
            for i in range(WIN_ROWS):
                at = (row + i, pl.ds(start, WIDE), slice(None))
                acc_ref[at] += part[i * WIDE : (i + 1) * WIDE]
        return carry

    lax.fori_loop(0, count // batch, step, 0)


def first_grid(row_ref, col_ref, live_ref, coef_ref, pos_ref, data_ref, acc_ref, *, batch):
    def clear(k, carry):
        acc_ref[k] = jnp.zeros(acc_ref.shape[1:], jnp.float32)
        return carry

    lax.fori_loop(0, acc_ref.shape[0], clear, 0)
    grid_slots(row_ref, col_ref, live_ref, coef_ref, pos_ref, data_ref, acc_ref, batch)


def second_grid(row_ref, col_ref, live_ref, coef_ref, pos_ref, data_ref, before_ref,
                inner_ref, own_ref, up_ref, down_ref, acc_ref, sem, *, batch):
    copy = pltpu.make_async_copy(before_ref, acc_ref, sem)
    copy.start()
    copy.wait()
    grid_slots(row_ref, col_ref, live_ref, coef_ref, pos_ref, data_ref, acc_ref, batch)

    def row_of(k):
        wrap = acc_ref[k, 0:WIDE, :] + acc_ref[k, PLANE:PAD, :]
        return jnp.concatenate([wrap, acc_ref[k, WIDE:PLANE, :]], axis=0)

    for k in range(2):
        up_ref[k] = row_of(k).astype(jnp.bfloat16)
        down_ref[k] = row_of(TILE_ROWS + 2 + k).astype(jnp.bfloat16)
        own_ref[k] = row_of(2 + k)
        own_ref[2 + k] = row_of(TILE_ROWS + k)

    def emit(k, carry):
        inner_ref[k] = row_of(k + 4).astype(jnp.bfloat16)
        return carry

    lax.fori_loop(0, TILE_ROWS - 4, emit, 0)


SMEM = pl.BlockSpec(memory_space=pltpu.SMEM)
VMEM = pl.BlockSpec(memory_space=pltpu.VMEM)
ANY = pl.BlockSpec(memory_space=pl.ANY)


def grid_first(rows, cols, live, coef, pos, data, batch=4):
    return pl.pallas_call(
        functools.partial(first_grid, batch=batch),
        out_shape=jax.ShapeDtypeStruct((TILE_ROWS + 4, PAD, 2 * LANES), jnp.float32),
        in_specs=[SMEM] * 4 + [VMEM] * 2,
        out_specs=VMEM,
        compiler_params=pltpu.CompilerParams(vmem_limit_bytes=32 * MB),
        cost_estimate=pl.CostEstimate(flops=3 * 10**9, bytes_accessed=20 * MB, transcendentals=0),
        name="grid_first",
    )(rows, cols, live, coef, pos, data)


def grid_second(rows, cols, live, coef, pos, data, before, batch=4):
    wide = 2 * LANES
    return pl.pallas_call(
        functools.partial(second_grid, batch=batch),
        out_shape=[
            jax.ShapeDtypeStruct((TILE_ROWS - 4, PLANE, wide), jnp.bfloat16),
            jax.ShapeDtypeStruct((4, PLANE, wide), jnp.float32),
            jax.ShapeDtypeStruct((2, PLANE, wide), jnp.bfloat16),
            jax.ShapeDtypeStruct((2, PLANE, wide), jnp.bfloat16),
        ],
        in_specs=[SMEM] * 4 + [VMEM] * 2 + [ANY],
        out_specs=[VMEM] * 4,
        scratch_shapes=[
            pltpu.VMEM((TILE_ROWS + 4, PAD, wide), jnp.float32),
            pltpu.SemaphoreType.DMA,
        ],
        compiler_params=pltpu.CompilerParams(vmem_limit_bytes=40 * MB),
        cost_estimate=pl.CostEstimate(flops=3 * 10**9, bytes_accessed=20 * MB, transcendentals=0),
        name="grid_second",
    )(rows, cols, live, coef, pos, data, before)


def interleave(pieces):
    lane = lax.broadcasted_iota(jnp.int32, pieces[0].shape, 1)
    p = [pieces[0]] + [pltpu.roll(pieces[k], (HALF * k) % LANES, 1) for k in range(1, 8)]
    return [
        jnp.where(lane < 80, p[0], p[1]),
        jnp.where(lane < 32, p[1], jnp.where(lane < 112, p[2], p[3])),
        jnp.where(lane < 64, p[3], p[4]),
        jnp.where(lane < 16, p[4], jnp.where(lane < 96, p[5], p[6])),
        jnp.where(lane < 48, p[6], p[7]),
    ]


def ky_rows(table_ref, plane_of, count, re_ref, im_ref):
    def transform(k, carry):
        plane = plane_of(k)
        re, im = plane[:, :LANES], plane[:, LANES:]
        stacked = jnp.concatenate(
            [plane, jnp.concatenate([-im, re], axis=1)], axis=0
        )
        out = jnp.dot(table_ref[...], stacked, preferred_element_type=jnp.float32)
        at = pl.ds(pl.multiple_of(k * PLANE, PLANE), PLANE)
        re_ref[at, :] = out[:, :LANES]
        im_ref[at, :] = out[:, LANES:]
        return carry

    lax.fori_loop(0, count, transform, 0)


def ky_inner(table_ref, grid_ref, out_ref, re_ref, im_ref):
    ky_rows(table_ref, lambda k: grid_ref[k], TILE_ROWS - 4, re_ref, im_ref)

    def block(d, carry):
        for b in range(5):
            halves = []
            for g in range(2):
                pieces = []
                for j in range(4):
                    at = pl.ds(g * 8 * PLANE + d * 20 + b * 4 + j, 8, stride=PLANE)
                    pieces += [re_ref[at, :], im_ref[at, :]]
                halves.append(jnp.concatenate(interleave(pieces), axis=1))
            out_ref[d, :, b * PLANE : (b + 1) * PLANE] = jnp.concatenate(halves, axis=0).astype(jnp.bfloat16)
        return carry

    lax.fori_loop(0, 32, block, 0)


def ky_edge(table_ref, own_ref, above_ref, below_ref, out_ref, grid_ref, re_ref, im_ref):
    for k in range(2):
        grid_ref[k] = (own_ref[k] + above_ref[k].astype(jnp.float32)).astype(jnp.bfloat16)
        grid_ref[2 + k] = (own_ref[2 + k] + below_ref[k].astype(jnp.float32)).astype(jnp.bfloat16)
    ky_rows(table_ref, lambda k: grid_ref[k], 4, re_ref, im_ref)

    def block(d, carry):
        for b in range(5):
            pieces = []
            for j in range(4):
                at = pl.ds(d * 20 + b * 4 + j, 4, stride=PLANE)
                pieces += [re_ref[at, :], im_ref[at, :]]
            out = jnp.concatenate(interleave(pieces), axis=1)
            out_ref[d, :, b * PLANE : (b + 1) * PLANE] = out.astype(jnp.bfloat16)
        return carry

    lax.fori_loop(0, 32, block, 0)


def transform_inner(table, grid):
    rows = TILE_ROWS - 4
    return pl.pallas_call(
        ky_inner,
        out_shape=jax.ShapeDtypeStruct((32, rows, 5 * PLANE), jnp.bfloat16),
        in_specs=[VMEM] * 2,
        out_specs=VMEM,
        scratch_shapes=[pltpu.VMEM((rows * PLANE, LANES), jnp.float32)] * 2,
        compiler_params=pltpu.CompilerParams(vmem_limit_bytes=40 * MB),
        cost_estimate=pl.CostEstimate(flops=8 * 10**9, bytes_accessed=10 * MB, transcendentals=0),
        name="ky_inner",
    )(table, grid)


def transform_edge(table, own, above, below):
    return pl.pallas_call(
        ky_edge,
        out_shape=jax.ShapeDtypeStruct((32, 4, 5 * PLANE), jnp.bfloat16),
        in_specs=[VMEM] * 4,
        out_specs=VMEM,
        scratch_shapes=[
            pltpu.VMEM((4, PLANE, 2 * LANES), jnp.bfloat16),
            pltpu.VMEM((4 * PLANE, LANES), jnp.float32),
            pltpu.VMEM((4 * PLANE, LANES), jnp.float32),
        ],
        compiler_params=pltpu.CompilerParams(vmem_limit_bytes=32 * MB),
        cost_estimate=pl.CostEstimate(flops=2 * 10**9, bytes_accessed=4 * MB, transcendentals=0),
        name="ky_edge",
    )(table, own, above, below)


def kx_block(inner_table_ref, edge_table_ref, inner_ref, edge_ref, out_ref):
    lane = lax.rem(lax.broadcasted_iota(jnp.int32, (320, PLANE), 1), 2 * HALF)
    real = lane < HALF
    for h in range(2):
        rows = slice(320 * h, 320 * (h + 1))

        def product(part):
            return jnp.dot(
                inner_table_ref[part, rows, :], inner_ref[...], preferred_element_type=jnp.float32
            ) + jnp.dot(edge_table_ref[part, rows, :], edge_ref[...], preferred_element_type=jnp.float32)

        first = product(0)
        second = product(1)
        ahead = pltpu.roll(second, PLANE - HALF, 1)
        behind = pltpu.roll(second, HALF, 1)
        out = first + jnp.where(real, -ahead, behind)
        out_ref[rows, :] = (out * (1.0 / PLANE)).astype(jnp.bfloat16)


def transform_kx(inner_table, edge_table, inner, edge):
    columns = inner.shape[1]
    return pl.pallas_call(
        kx_block,
        grid=(columns // PLANE,),
        out_shape=jax.ShapeDtypeStruct((PLANE, columns), jnp.bfloat16),
        in_specs=[
            VMEM,
            VMEM,
            pl.BlockSpec((512, PLANE), lambda n: (0, n)),
            pl.BlockSpec((128, PLANE), lambda n: (0, n)),
        ],
        out_specs=pl.BlockSpec((PLANE, PLANE), lambda n: (0, n)),
        compiler_params=pltpu.CompilerParams(vmem_limit_bytes=40 * MB),
        cost_estimate=pl.CostEstimate(flops=8 * 10**9, bytes_accessed=10 * MB, transcendentals=0),
        name="kx",
    )(inner_table, edge_table, inner, edge)


def tables(n):
    idx = jnp.arange(n, dtype=jnp.int32)
    phase = (idx[:, None] * idx[None, :] % n).astype(jnp.float32) * (2.0 * math.pi / n)
    return (jnp.cos(phase).astype(jnp.bfloat16), jnp.sin(phase).astype(jnp.bfloat16))


def make_tables():
    cos_tab, sin_tab = tables(PLANE)
    ky_table = jnp.concatenate([cos_tab, sin_tab], axis=1)
    both = jnp.stack([cos_tab, sin_tab]).reshape(2, PLANE, 32, TILE_ROWS)
    inner_table = both[..., 2:18].reshape(2, PLANE, 512)
    edge_table = jnp.concatenate([both[..., 0:2], both[..., 18:20]], axis=-1).reshape(2, PLANE, 128)
    return ky_table, inner_table, edge_table


def neighbour(value, steps):
    count = lax.axis_size("tile")
    pairs = [(source, (source + steps) % count) for source in range(count)]
    return lax.ppermute(value, "tile", pairs)


def body(coil_data, frame_of, basis, sample_pos, window_at, live_count):
    axes = ("kz", "tile")
    devices = 256
    data = coil_data.reshape(devices, 2, 16, LANES)
    arrived = [
        lax.all_to_all(data[:, s], axes, split_axis=0, concat_axis=0, tiled=True) for s in range(2)
    ]
    me = lax.axis_index("kz") * lax.axis_size("tile") + lax.axis_index("tile")
    gathered = lax.all_gather(frame_of.reshape(4, LANES), axes, axis=0, tiled=False)
    frames = lax.dynamic_slice(gathered.reshape(devices, devices, 2), (0, me, 0), (devices, 1, 2))
    frames = frames.reshape(devices, 2)
    coef = basis[frames.T.reshape(-1)].astype(jnp.float32).reshape(2, devices * 10)
    window = window_at.reshape(devices, 2, 2)
    live = (jnp.arange(2)[:, None] < live_count.reshape(1, devices)).astype(jnp.float32)
    pos = sample_pos.reshape(devices, 2, 2, LANES)

    def slot(s):
        return window[:, s, 0], window[:, s, 1], live[s], coef[s], pos[:, s], arrived[s]

    ky_table, inner_table, edge_table = make_tables()
    before = grid_first(*slot(0))
    inner, own, up, down = grid_second(*slot(1), before)
    from_above = neighbour(down, 1)
    from_below = neighbour(up, -1)
    mid_inner = transform_inner(ky_table, inner)
    mid_inner = lax.all_to_all(mid_inner, "tile", split_axis=0, concat_axis=0, tiled=True)
    mid_edge = transform_edge(ky_table, own, from_above, from_below)
    mid_edge = lax.all_to_all(mid_edge, "tile", split_axis=0, concat_axis=0, tiled=True)
    image = transform_kx(
        inner_table, edge_table, mid_inner.reshape(512, 5 * PLANE), mid_edge.reshape(128, 5 * PLANE)
    )
    return image[None]


def solution(mesh):
    return jax.shard_map(
        body,
        mesh=mesh,
        in_specs=(
            P("kz", "tile", None, None, None, None, None),
            P("kz", "tile", None, None, None),
            P(),
            P("kz", "tile", None, None, None, None, None),
            P("kz", "tile", None, None, None, None),
            P("kz", "tile", None, None),
        ),
        out_specs=P("kz", None, "tile"),
        check_vma=False,
    )
```

time: 987 us -> 360 us (0.36)
  other arithmetic: 499 us -> 19.5 us
  blocking collectives: 212 us -> 87.4 us
  matrix products: 106 us -> 0 us
  Pallas kernels: 0 us -> 86.1 us
  local copies, waits for them, and re-layouts: 90.2 us -> 30.3 us
  starting transfers between devices: 8.43 us -> 42.5 us
  waiting for transfers between devices: 68.1 us -> 87.4 us
    while x32 -> x0, other arithmetic: 447 us -> none
    all_to_all x2 -> x0, blocking collectives: 212 us -> none  [the longest x1 185 us: body(): lax.all_to_all(mid, 'tile', split_axis=1, concat_axis=0, tiled=True)]
    all_gather x0 -> x1, blocking collectives: none -> 87.4 us  [body(): lax.all_gather(frame_of.reshape(4, LANES), axes, axis=0, tiled=False)]
    pallas_call x0 -> x5, Pallas kernels: none -> 86.1 us  [the longest x1 27.3 us: grid_second(): pl.pallas_call(functools.partial(second_grid, batch=batch), out_shape=[ja...]
    reshape x8 -> x0, matrix products: 53.7 us -> none  [step(): contrib.reshape(-1, width)]
    unnamed x4 -> x0, matrix products: 52.2 us -> none
    all_to_all x1 -> x4, starting transfers between devices: 6.31 us -> 40.5 us  [the longest x2 20.9 us: body(): lax.all_to_all(data[:, s], axes, split_axis=0, concat_axis=0, tiled=True)]
    all_to_all x1 -> x4, waiting for transfers between devices: 49.1 us -> 81.1 us  [the longest x1 49.9 us: body(): lax.all_to_all(mid_inner, 'tile', split_axis=0, concat_axis=0, tiled=True)]
  transfers between devices with their start and end apart: 3 -> 6, of which waited for: 3 -> 4; matrix products, arithmetic and copies ran while one was open for 0% -> 9% of each run, Pallas kernels for 0% -> 11%
where the time goes in v1:
time: 360 us; the launch traced here: 353 us
  waiting for transfers between devices  87.4 us (24%)
  blocking collectives  87.4 us (24%)
  Pallas kernels  86.1 us (24%)
  starting transfers between devices  42.5 us (12%)
  local copies, waits for them, and re-layouts  30.3 us (8%)
  other arithmetic  19.5 us (5%)
    all_gather x1, blocking collectives, body(): lax.all_gather(frame_of.reshape(4, LANES), axes, axis=0, tiled=False)  87.4 us
    all_to_all x1, waiting for transfers between devices, body(): lax.all_to_all(mid_inner, 'tile', split_axis=0, concat_axis=0, tiled=True)  49.9 us
    all_to_all x2, waiting for transfers between devices, body(): lax.all_to_all(data[:, s], axes, split_axis=0, concat_axis=0, tiled=True)  31.2 us
    pallas_call x1, Pallas kernels, grid_second(): pl.pallas_call(functools.partial(second_grid, batch=batch), out_shape=[ja...  27.3 us
    pallas_call x1, Pallas kernels, grid_first(): pl.pallas_call(functools.partial(first_grid, batch=batch), out_shape=jax....  21.8 us
    all_to_all x2, starting transfers between devices, body(): lax.all_to_all(data[:, s], axes, split_axis=0, concat_axis=0, tiled=True)  20.9 us
    pallas_call x1, Pallas kernels, transform_inner(): pl.pallas_call(ky_inner, out_shape=jax.ShapeDtypeStruct((32, rows, 5 * PL...  18.4 us
    unnamed x35, local copies, waits for them, and re-layouts  18.4 us
  transfers between devices with their start and end apart: 6, of which 4 were waited for; matrix products, arithmetic and copies ran while one was open for 9% of the time, Pallas kernels for 11%

profile of v1, /device:TPU:32, one launch (start us, length us, event | category | flops | bytes accessed | tf_op | source)
XLA Modules:
  0.0 353.5 jit_solution(18136926010478785730)
XLA Ops:
  0.0 2.1 copy.25
  2.1 1.7 slice_bitcast_fusion
  3.8 14.4 %all-to-all-start.1 = ((bf16[256,16,128]{2,1,0:T(8,128)(2,1)}), bf16[256,16,128]{2,1,0:T(8,128)(2,1)S(1)}, u32[]{:S(2)}, u32[]{:S(2)}) async-start(bf16[256,16,128]{2,1,0:T(8,128)(2,1)} %get-tuple-element.13), calls=%async_computation.1 | async-start | bytes 2097152 | tf_op jit(solution)/shard_map/all_to_all | solution.py:300
  18.5 31.2 %all-to-all-done.1.data_ref = bf16[256,16,128]{2,1,0:T(8,128)(2,1)S(1)} async-done(((bf16[256,16,128]{2,1,0:T(8,128)(2,1)}), bf16[256,16,128]{2,1,0:T(8,128)(2,1)S(1)}, u32[]{:S(2)}, u32[]{:S(2)}) %all-to-all-start.1) | async-done | bytes 1048608 | tf_op jit(solution)/shard_map/all_to_all | solution.py:300
  49.7 6.5 %all-to-all-start = ((bf16[256,16,128]{2,1,0:T(8,128)(2,1)}), bf16[256,16,128]{2,1,0:T(8,128)(2,1)S(1)}, u32[]{:S(2)}, u32[]{:S(2)}) async-start(bf16[256,16,128]{2,1,0:T(8,128)(2,1)} %get-tuple-element.14), calls=%async_computation | async-start | bytes 2097152 | tf_op jit(solution)/shard_map/all_to_all | solution.py:300
  56.2 87.4 %all_gather.3 = s32[256,4,128]{2,1,0:T(4,128)S(1)} all-gather(s32[1,4,128]{2,1,0:T(4,128)S(1)} %all_gather_reshape.3), channel_id=1, replica_groups=mesh['kz'=8,'tile'=32] {'kz','tile'}, dimensions={0}, use_global_device_ids=true | all-gather | bytes 526336 | tf_op jit(solution)/shard_map/all_gather | solution.py:303
  144.5 1.3 gather_fusion
  146.7 21.8 %grid_first.1.before_ref = f32[24,680,256]{2,1,0:T(8,128)S(1)} custom-call(s32[256]{0:T(256)S(1)} %bitcast.45, s32[256]{0:T(256)S(1)} %bitcast.44, f32[256]{0:T(256)S(1)} %bitcast.41, f32[2560]{0:T(1024)S(1)} %squeeze.45.coef_ref, f32[256,2,128]{2,1,0:T(2,128)S(1)} %get-tuple-element.15.pos_ref, bf16[256,16,128]{2,1,0:T(8,128)(2,1)S(1)} %all-to-all-done.1.data_ref), custom_call_target="tpu_custom_call" | custom-call | flops 3000000000 | bytes 20971520 | tf_op jit(solution)/shard_map/grid_first/pallas_call | solution.py:107
  168.5 5.7 %copy-done = f32[24,680,256]{2,1,0:T(8,128)} copy-done((f32[24,680,256]{2,1,0:T(8,128)}, f32[24,680,256]{2,1,0:T(8,128)S(1)}, u32[]{:S(2)}) %copy-start) | copy-done | bytes 16711704
  174.2 27.3 %grid_second.1 = (bf16[16,640,256]{2,1,0:T(8,128)(2,1)S(1)}, f32[4,640,256]{2,1,0:T(8,128)S(1)}, bf16[2,640,256]{2,1,0:T(8,128)(2,1)S(1)}, bf16[2,640,256]{2,1,0:T(8,128)(2,1)S(1)}) custom-call(s32[256]{0:T(256)S(1)} %bitcast.43, s32[256]{0:T(256)S(1)} %bitcast.42, f32[256]{0:T(256)S(1)} %bitcast.40, f32[2560]{0:T(1024)S(1)} %squeeze.39.coef_ref, ...), custom_call_target="tpu_custom_call" | custom-call | flops 3000000000 | bytes 20971520 | tf_op jit(solution)/shard_map/grid_second/pallas_call | solution.py:120
  201.5 2.3 copy-done.4
  203.9 1.9 collective-permute-start
  205.9 6.9 %sine_convert_fusion.1 = (bf16[640,640]{1,0:T(8,128)(2,1)S(1)}, bf16[640,640]{1,0:T(8,128)(2,1)S(1)}) fusion(), kind=kLoop, calls=%fused_computation.18 | loop fusion | flops 4505600 | bytes 1638400 | tf_op jit(solution)/shard_map/convert_element_type | solution.py:277
  212.9 5.0 %collective-permute-done.above_ref = bf16[2,640,256]{2,1,0:T(8,128)(2,1)S(1)} collective-permute-done((bf16[2,640,256]{2,1,0:T(8,128)(2,1)S(1)}, bf16[2,640,256]{2,1,0:T(8,128)(2,1)S(1)}, u32[]{:S(2)}, u32[]{:S(2)}) %collective-permute-start) | collective-permute-done | bytes 655392 | tf_op jit(solution)/shard_map/ppermute | solution.py:292
  218.0 1.2 collective-permute-done.1.below_ref
  219.2 7.0 %ky_edge.1 = bf16[32,4,3200]{2,1,0:T(4,128)(2,1)} custom-call(bf16[640,1280]{1,0:T(8,128)(2,1)S(1)} %pad_maximum_fusion.table_ref, f32[4,640,256]{2,1,0:T(8,128)S(1)} %get-tuple-element.10.own_ref, bf16[2,640,256]{2,1,0:T(8,128)(2,1)S(1)} %collective-permute-done.above_ref, bf16[2,640,256]{2,1,0:T(8,128)(2,1)S(1)} %collective-permute-done.1.below_ref), custom_call_target="tpu_custom_call" | custom-call | flops 2000000000 | bytes 4194304 | tf_op jit(solution)/shard_map/ky_edge/pallas_call | solution.py:220
  226.2 9.8 %all-to-all-start.3 = ((bf16[32,4,3200]{2,1,0:T(4,128)(2,1)}), bf16[32,4,3200]{2,1,0:T(4,128)(2,1)S(1)}, u32[]{:S(2)}, u32[]{:S(2)}) async-start(bf16[32,4,3200]{2,1,0:T(4,128)(2,1)} %ky_edge.1), calls=%async_computation.3 | async-start | bytes 1638400 | tf_op jit(solution)/shard_map/all_to_all | solution.py:322
  236.0 2.5 copy-done.5
  238.5 18.4 %ky_inner.1 = bf16[32,16,3200]{2,1,0:T(8,128)(2,1)} custom-call(bf16[640,1280]{1,0:T(8,128)(2,1)S(1)} %pad_maximum_fusion.table_ref, bf16[16,640,256]{2,1,0:T(8,128)(2,1)S(1)} %copy-done.5), custom_call_target="tpu_custom_call" | custom-call | flops 8000000000 | bytes 10485760 | tf_op jit(solution)/shard_map/ky_inner/pallas_call | solution.py:207
  256.9 0.9 copy-done.8
  257.8 9.8 %all-to-all-start.2 = ((bf16[32,16,3200]{2,1,0:T(8,128)(2,1)}), bf16[32,16,3200]{2,1,0:T(8,128)(2,1)S(1)}, u32[]{:S(2)}, u32[]{:S(2)}) async-start(bf16[32,16,3200]{2,1,0:T(8,128)(2,1)} %ky_inner.1), calls=%async_computation.2 | async-start | bytes 6553600 | tf_op jit(solution)/shard_map/all_to_all | solution.py:320
  267.6 8.8 %sine_convert_fusion = (bf16[1,640,32,20]{1,3,2,0:T(8,128)(2,1)S(1)}, bf16[1,640,32,20]{1,3,2,0:T(8,128)(2,1)S(1)}) fusion(s32[32,20]{1,0:T(8,128)S(1)} %multiply_add_fusion), kind=kLoop, calls=%fused_computation.9 | loop fusion | flops 4505600 | bytes 1640960 | tf_op jit(solution)/shard_map/convert_element_type | solution.py:277
  277.7 1.1 copy.19
  278.8 1.9 copy.27.edge_table_ref
  280.7 3.2 fusion.10
  283.9 2.4 copy.26.inner_table_ref
  286.3 2.3 reshape.149.edge_ref
  288.6 49.9 %all-to-all-done.2 = bf16[32,16,3200]{2,1,0:T(8,128)(2,1)S(1)} async-done(((bf16[32,16,3200]{2,1,0:T(8,128)(2,1)}), bf16[32,16,3200]{2,1,0:T(8,128)(2,1)S(1)}, u32[]{:S(2)}, u32[]{:S(2)}) %all-to-all-start.2) | async-done | bytes 3276832 | tf_op jit(solution)/shard_map/all_to_all | solution.py:320
  338.6 1.3 copy-done.1
  339.9 1.1 copy-done.2
  341.0 1.0 copy-done.3
  342.0 11.5 %kx.1 = bf16[640,3200]{1,0:T(8,128)(2,1)} custom-call(bf16[2,640,512]{2,1,0:T(8,128)(2,1)S(1)} %copy-done.1, bf16[2,640,128]{2,1,0:T(8,128)(2,1)S(1)} %copy-done.3, bf16[512,3200]{1,0:T(8,128)(2,1)S(1)} %bitcast.39, bf16[128,3200]{1,0:T(8,128)(2,1)S(1)} %copy-done.2), custom_call_target="tpu_custom_call" | custom-call | flops 8000000000 | bytes 10485760 | tf_op jit(solution)/shard_map/kx/pallas_call | solution.py:257
  (48 shorter events, 3.3 us)
Async XLA Ops:
  3.8 14.4 %copy-start.12 = (s32[1,1,8,32,2]{3,4,2,1,0:T(2,128)S(1)}, s32[1,1,8,32,2]{3,4,2,1,0:T(2,128)}, u32[]{:S(2)}) copy-start(s32[1,1,8,32,2]{3,4,2,1,0:T(2,128)} %param.7) | copy-start | bytes 6148
  3.8 45.9 %all-to-all-start.1 = ((bf16[256,16,128]{2,1,0:T(8,128)(2,1)}), bf16[256,16,128]{2,1,0:T(8,128)(2,1)S(1)}, u32[]{:S(2)}, u32[]{:S(2)}) async-start(bf16[256,16,128]{2,1,0:T(8,128)(2,1)} %get-tuple-element.13), calls=%async_computation.1 | async-start | bytes 2097152 | tf_op jit(solution)/shard_map/all_to_all | solution.py:300
  49.7 94.5 %copy-start.10 = (bf16[1000,10]{0,1:T(8,128)(2,1)S(1)}, bf16[1000,10]{0,1:T(8,128)(2,1)}, u32[]{:S(2)}) copy-start(bf16[1000,10]{0,1:T(8,128)(2,1)} %param.8) | copy-start | bytes 60004
  49.7 124.5 %all-to-all-start = ((bf16[256,16,128]{2,1,0:T(8,128)(2,1)}), bf16[256,16,128]{2,1,0:T(8,128)(2,1)S(1)}, u32[]{:S(2)}, u32[]{:S(2)}) async-start(bf16[256,16,128]{2,1,0:T(8,128)(2,1)} %get-tuple-element.14), calls=%async_computation | async-start | bytes 2097152 | tf_op jit(solution)/shard_map/all_to_all | solution.py:300
  143.6 2.4 copy-start.11
  143.8 2.5 copy-start.13
  144.2 1.9 copy-start.9
  168.5 5.7 %copy-start = (f32[24,680,256]{2,1,0:T(8,128)}, f32[24,680,256]{2,1,0:T(8,128)S(1)}, u32[]{:S(2)}) copy-start(f32[24,680,256]{2,1,0:T(8,128)S(1)} %grid_first.1.before_ref) | copy-start | bytes 50135044
  201.5 2.3 copy-start.4
  203.9 14.1 %collective-permute-start = (bf16[2,640,256]{2,1,0:T(8,128)(2,1)S(1)}, bf16[2,640,256]{2,1,0:T(8,128)(2,1)S(1)}, u32[]{:S(2)}, u32[]{:S(2)}) collective-permute-start(bf16[2,640,256]{2,1,0:T(8,128)(2,1)S(1)} %get-tuple-element.11), channel_id=1, source_target_pairs={{0,1},{1,2},{2,3},{3,4},{4,5},{5,6},{6,7},{7,8},{8,9},{9,10},{10,1... | collective-permute-start | bytes 1966088 | tf_op jit(solution)/shard_map/ppermute | solution.py:292
  205.7 13.5 %collective-permute-start.1 = (bf16[2,640,256]{2,1,0:T(8,128)(2,1)S(1)}, bf16[2,640,256]{2,1,0:T(8,128)(2,1)S(1)}, u32[]{:S(2)}, u32[]{:S(2)}) collective-permute-start(bf16[2,640,256]{2,1,0:T(8,128)(2,1)S(1)} %get-tuple-element.12), channel_id=1, source_target_pairs={{0,31},{1,0},{2,1},{3,2},{4,3},{5,4},{6,5},{7,6},{8,7},{9,8},{10,9... | collective-permute-start | bytes 1966088 | tf_op jit(solution)/shard_map/ppermute | solution.py:292
  226.2 30.7 %all-to-all-start.3 = ((bf16[32,4,3200]{2,1,0:T(4,128)(2,1)}), bf16[32,4,3200]{2,1,0:T(4,128)(2,1)S(1)}, u32[]{:S(2)}, u32[]{:S(2)}) async-start(bf16[32,4,3200]{2,1,0:T(4,128)(2,1)} %ky_edge.1), calls=%async_computation.3 | async-start | bytes 1638400 | tf_op jit(solution)/shard_map/all_to_all | solution.py:322
  236.0 2.5 copy-start.5
  256.9 0.9 copy-start.8
  257.8 80.7 %all-to-all-start.2 = ((bf16[32,16,3200]{2,1,0:T(8,128)(2,1)}), bf16[32,16,3200]{2,1,0:T(8,128)(2,1)S(1)}, u32[]{:S(2)}, u32[]{:S(2)}) async-start(bf16[32,16,3200]{2,1,0:T(8,128)(2,1)} %ky_inner.1), calls=%async_computation.2 | async-start | bytes 6553600 | tf_op jit(solution)/shard_map/all_to_all | solution.py:320
  276.5 1.0 copy-start.6
  276.5 1.2 copy-start.7
  338.6 1.3 copy-start.1
  339.9 1.1 copy-start.2
  341.0 1.0 copy-start.3

commit v2 on v1

v2 whole, which is shorter than its diff:
```python
import functools
import math

import jax
import jax.numpy as jnp
from jax import lax
from jax.experimental import pallas as pl
from jax.experimental.pallas import tpu as pltpu
from jax.sharding import PartitionSpec as P
import ml_dtypes
import numpy as np

PLANE = 640
WIN_ROWS = 4
WIN_COLS = 32
TILE_ROWS = 20
WIDE = 40
PAD = 680
LANES = 128
HALF = 80
MB = 1024 * 1024


def taper(dist):
    inner = 1.0 - (dist * (1.0 / 1.5)) * (dist * (1.0 / 1.5))
    inner = jnp.maximum(inner, 0.0)
    return inner * inner


def grid_slots(row_ref, col_ref, live_ref, coef_ref, pos_ref, data_ref, acc_ref, batch):
    count = data_ref.shape[0]
    row_cell = lax.broadcasted_iota(jnp.int32, (8, LANES), 0)
    col_cell = lax.broadcasted_iota(jnp.int32, (WIDE, LANES), 0)
    zero = jnp.zeros((LANES - HALF, LANES), jnp.bfloat16)

    def contribution(s):
        col0 = col_ref[s]
        shift = jnp.bitwise_and(col0, 7)
        place = pos_ref[s]
        u = place[0:1, :]
        v = place[1:2, :]
        row_k = taper(row_cell.astype(jnp.float32) - u) * live_ref[s]
        col_k = taper((col_cell - shift).astype(jnp.float32) - v)
        weight = jnp.concatenate([row_k[i : i + 1, :] * col_k for i in range(WIN_ROWS)], axis=0)
        weight = weight.astype(jnp.bfloat16)
        data = data_ref[s].astype(jnp.float32)
        re, im = data[0:8], data[8:16]
        scale = [coef_ref[s * 10 + r] for r in range(10)]
        re = jnp.concatenate([re * c for c in scale], axis=0).astype(jnp.bfloat16)
        im = jnp.concatenate([im * c for c in scale], axis=0).astype(jnp.bfloat16)
        values = jnp.concatenate([re, zero, im, zero], axis=0)
        return lax.dot_general(
            weight, values, (((1,), (1,)), ((), ())), preferred_element_type=jnp.float32
        )

    def step(b, carry):
        slots = [b * batch + k for k in range(batch)]
        parts = [contribution(s) for s in slots]
        for s, part in zip(slots, parts):
            row = row_ref[s] + 2
            start = pl.multiple_of(jnp.bitwise_and(col_ref[s], -8), 8)
            for i in range(WIN_ROWS):
                at = (row + i, pl.ds(start, WIDE), slice(None))
                acc_ref[at] += part[i * WIDE : (i + 1) * WIDE]
        return carry

    lax.fori_loop(0, count // batch, step, 0)


def grid_kernel(row_ref, col_ref, live_ref, coef_ref, pos_ref, data_ref,
                inner_ref, own_ref, up_ref, down_ref, acc_ref, *, batch):
    def clear(k, carry):
        acc_ref[k] = jnp.zeros(acc_ref.shape[1:], jnp.float32)
        return carry

    lax.fori_loop(0, acc_ref.shape[0], clear, 0)
    grid_slots(row_ref, col_ref, live_ref, coef_ref, pos_ref, data_ref, acc_ref, batch)

    def row_of(k):
        wrap = acc_ref[k, 0:WIDE, :] + acc_ref[k, PLANE:PAD, :]
        return jnp.concatenate([wrap, acc_ref[k, WIDE:PLANE, :]], axis=0)

    for k in range(2):
        up_ref[k] = row_of(k).astype(jnp.bfloat16)
        down_ref[k] = row_of(TILE_ROWS + 2 + k).astype(jnp.bfloat16)
        own_ref[k] = row_of(2 + k)
        own_ref[2 + k] = row_of(TILE_ROWS + k)

    def emit(k, carry):
        inner_ref[k] = row_of(k + 4).astype(jnp.bfloat16)
        return carry

    lax.fori_loop(0, TILE_ROWS - 4, emit, 0)


SMEM = pl.BlockSpec(memory_space=pltpu.SMEM)
VMEM = pl.BlockSpec(memory_space=pltpu.VMEM)


def grid_tile(rows, cols, live, coef, pos, data, batch=4):
    wide = 2 * LANES
    return pl.pallas_call(
        functools.partial(grid_kernel, batch=batch),
        out_shape=[
            jax.ShapeDtypeStruct((TILE_ROWS - 4, PLANE, wide), jnp.bfloat16),
            jax.ShapeDtypeStruct((4, PLANE, wide), jnp.float32),
            jax.ShapeDtypeStruct((2, PLANE, wide), jnp.bfloat16),
            jax.ShapeDtypeStruct((2, PLANE, wide), jnp.bfloat16),
        ],
        in_specs=[SMEM] * 4 + [VMEM] * 2,
        out_specs=[VMEM] * 4,
        scratch_shapes=[pltpu.VMEM((TILE_ROWS + 4, PAD, wide), jnp.float32)],
        compiler_params=pltpu.CompilerParams(vmem_limit_bytes=40 * MB),
        cost_estimate=pl.CostEstimate(flops=6 * 10**9, bytes_accessed=20 * MB, transcendentals=0),
        name="grid_tile",
    )(rows, cols, live, coef, pos, data)


def interleave(pieces):
    lane = lax.broadcasted_iota(jnp.int32, pieces[0].shape, 1)
    p = [pieces[0]] + [pltpu.roll(pieces[k], (HALF * k) % LANES, 1) for k in range(1, 8)]
    return [
        jnp.where(lane < 80, p[0], p[1]),
        jnp.where(lane < 32, p[1], jnp.where(lane < 112, p[2], p[3])),
        jnp.where(lane < 64, p[3], p[4]),
        jnp.where(lane < 16, p[4], jnp.where(lane < 96, p[5], p[6])),
        jnp.where(lane < 48, p[6], p[7]),
    ]


def mid_kernel(ky_ref, inner_table_ref, edge_table_ref, grid_ref, own_ref, up_ref, down_ref, out_ref,
               send_in, send_ed, recv_in, recv_ed, halo, rot, edge_grid, edge_rot, re_ref, im_ref, edge_kx,
               halo_send, halo_recv, send_sem_in, recv_sem_in, send_sem_ed, recv_sem_ed):
    count = lax.axis_size("tile")
    me = lax.axis_index("tile")
    above = lax.rem(me + count - 1, count)
    below = lax.rem(me + 1, count)
    stages = ky_ref.shape[0]
    inner_rows = TILE_ROWS - 4

    barrier = pltpu.get_barrier_semaphore()

    def greet(k, carry):
        pl.semaphore_signal(
            barrier, inc=1, device_id={"tile": lax.rem(me + k, count)}, device_id_type=pl.DeviceIdType.MESH
        )
        return carry

    lax.fori_loop(1, count, greet, 0)
    pl.semaphore_wait(barrier, count - 1)

    def halo_copy(source, way, peer):
        return pltpu.make_async_remote_copy(
            src_ref=source, dst_ref=halo.at[way], send_sem=halo_send.at[way], recv_sem=halo_recv.at[way],
            device_id={"tile": peer}, device_id_type=pl.DeviceIdType.MESH,
        )

    to_below = halo_copy(down_ref, 0, below)
    to_above = halo_copy(up_ref, 1, above)
    to_below.start()
    to_above.start()

    def turned(plane):
        return jnp.concatenate([-plane[:, LANES:], plane[:, :LANES]], axis=1)

    def turn(k, carry):
        rot[k] = turned(grid_ref[k])
        return carry

    lax.fori_loop(0, inner_rows, turn, 0)

    def rows_of(b, k, plane_ref, turned_ref):
        out = jnp.dot(ky_ref[b, :, :PLANE], plane_ref[k], preferred_element_type=jnp.float32)
        out += jnp.dot(ky_ref[b, :, PLANE:], turned_ref[k], preferred_element_type=jnp.float32)
        at = pl.ds(pl.multiple_of(k * LANES, LANES), LANES)
        re_ref[at, :] = out[:, :LANES]
        im_ref[at, :] = out[:, LANES:]

    def pieces_of(start, size):
        pieces = []
        for j in range(4):
            at = pl.ds(start + j, size, stride=LANES)
            pieces += [re_ref[at, :], im_ref[at, :]]
        return jnp.concatenate(interleave(pieces), axis=1)

    def send_all(b, send, recv, send_sem, recv_sem):
        recv[b, me] = send[b, me]

        def to_peer(k, carry):
            peer = lax.rem(me + k, count)
            pltpu.make_async_remote_copy(
                src_ref=send.at[b, peer], dst_ref=recv.at[b, me],
                send_sem=send_sem.at[b], recv_sem=recv_sem.at[b],
                device_id={"tile": peer}, device_id_type=pl.DeviceIdType.MESH,
            ).start()
            return carry

        lax.fori_loop(1, count, to_peer, 0)

    def stage(b, carry):
        def inner_row(k, carry):
            rows_of(b, k, grid_ref, rot)
            return carry

        lax.fori_loop(0, inner_rows, inner_row, 0)

        def inner_pack(d, carry):
            halves = [pieces_of(g * 8 * LANES + d * 4, 8) for g in range(2)]
            send_in[b, d] = jnp.concatenate(halves, axis=0).astype(jnp.bfloat16)
            return carry

        lax.fori_loop(0, count, inner_pack, 0)
        send_all(b, send_in, recv_in, send_sem_in, recv_sem_in)

        @pl.when(b == 0)
        def _():
            to_below.wait()
            to_above.wait()
            for k in range(2):
                edge_grid[k] = (own_ref[k] + halo[0, k].astype(jnp.float32)).astype(jnp.bfloat16)
                edge_grid[2 + k] = (own_ref[2 + k] + halo[1, k].astype(jnp.float32)).astype(jnp.bfloat16)
            for k in range(4):
                edge_rot[k] = turned(edge_grid[k])

        def edge_row(k, carry):
            rows_of(b, k, edge_grid, edge_rot)
            return carry

        lax.fori_loop(0, 4, edge_row, 0)

        def edge_pack(d, carry):
            send_ed[b, d] = pieces_of(d * 4, 4).astype(jnp.bfloat16)
            return carry

        lax.fori_loop(0, count, edge_pack, 0)
        send_all(b, send_ed, recv_ed, send_sem_ed, recv_sem_ed)
        return carry

    lax.fori_loop(0, stages, stage, 0)

    lane = lax.rem(lax.broadcasted_iota(jnp.int32, (320, PLANE), 1), 2 * HALF)
    real = lane < HALF

    def others(b, ref, send_sem, recv_sem):
        return pltpu.make_async_remote_copy(
            src_ref=ref.at[b, pl.ds(0, count - 1)], dst_ref=ref.at[b, pl.ds(0, count - 1)],
            send_sem=send_sem.at[b], recv_sem=recv_sem.at[b],
            device_id={"tile": below}, device_id_type=pl.DeviceIdType.MESH,
        )

    def finish(b, carry):
        others(b, recv_in, send_sem_in, recv_sem_in).wait_recv()
        others(b, recv_ed, send_sem_ed, recv_sem_ed).wait_recv()

        def lift(s, carry):
            pair = [recv_ed[b, 2 * s + k].astype(jnp.float32) for k in range(2)]
            edge_kx[pl.ds(pl.multiple_of(8 * s, 8), 8), :] = jnp.concatenate(pair, axis=0)
            return carry

        lax.fori_loop(0, count // 2, lift, 0)
        inner = recv_in[b].reshape(count * inner_rows, PLANE)
        edge = edge_kx[...].astype(jnp.bfloat16)
        for h in range(2):
            rows = slice(320 * h, 320 * (h + 1))

            def product(part):
                return jnp.dot(
                    inner_table_ref[part, rows, :], inner, preferred_element_type=jnp.float32
                ) + jnp.dot(edge_table_ref[part, rows, :], edge, preferred_element_type=jnp.float32)

            first = product(0)
            second = product(1)
            ahead = pltpu.roll(second, PLANE - HALF, 1)
            behind = pltpu.roll(second, HALF, 1)
            out = first + jnp.where(real, -ahead, behind)
            at = pl.ds(pl.multiple_of(b * PLANE, PLANE), PLANE)
            out_ref[rows, at] = (out * (1.0 / PLANE)).astype(jnp.bfloat16)
        return carry

    lax.fori_loop(0, stages, finish, 0)

    def sent(b, carry):
        others(b, send_in, send_sem_in, recv_sem_in).wait_send()
        others(b, send_ed, send_sem_ed, recv_sem_ed).wait_send()
        return carry

    lax.fori_loop(0, stages, sent, 0)


def transform_plane(ky_table, inner_table, edge_table, grid, own, up, down):
    stages, count, rows, wide = 5, 32, TILE_ROWS - 4, 2 * LANES
    bf16, f32 = jnp.bfloat16, jnp.float32
    dma = pltpu.SemaphoreType.DMA
    return pl.pallas_call(
        mid_kernel,
        out_shape=jax.ShapeDtypeStruct((PLANE, stages * PLANE), bf16),
        in_specs=[VMEM] * 7,
        out_specs=VMEM,
        scratch_shapes=[
            pltpu.VMEM((stages, count, rows, PLANE), bf16),
            pltpu.VMEM((stages, count, 4, PLANE), bf16),
            pltpu.VMEM((stages, count, rows, PLANE), bf16),
            pltpu.VMEM((stages, count, 4, PLANE), bf16),
            pltpu.VMEM((2, 2, PLANE, wide), bf16),
            pltpu.VMEM((rows, PLANE, wide), bf16),
            pltpu.VMEM((4, PLANE, wide), bf16),
            pltpu.VMEM((4, PLANE, wide), bf16),
            pltpu.VMEM((rows * LANES, LANES), f32),
            pltpu.VMEM((rows * LANES, LANES), f32),
            pltpu.VMEM((4 * count, PLANE), f32),
            dma((2,)), dma((2,)), dma((stages,)), dma((stages,)), dma((stages,)), dma((stages,)),
        ],
        compiler_params=pltpu.CompilerParams(
            vmem_limit_bytes=42 * MB, collective_id=0, has_side_effects=True
        ),
        cost_estimate=pl.CostEstimate(flops=20 * 10**9, bytes_accessed=20 * MB, transcendentals=0),
        name="plane",
    )(ky_table, inner_table, edge_table, grid, own, up, down)


def make_tables():
    idx = np.arange(PLANE)
    phase = (idx[:, None] * idx[None, :] % PLANE).astype(np.float32) * np.float32(2.0 * math.pi / PLANE)
    cos_tab = np.cos(phase).astype(ml_dtypes.bfloat16)
    sin_tab = np.sin(phase).astype(ml_dtypes.bfloat16)
    ky_table = np.concatenate([cos_tab, sin_tab], axis=1)
    ky_table = ky_table.reshape(32, 5, 4, 2 * PLANE).transpose(1, 0, 2, 3).reshape(5, LANES, 2 * PLANE)
    both = np.stack([cos_tab, sin_tab]).reshape(2, PLANE, 32, TILE_ROWS)
    inner_table = both[..., 2:18].reshape(2, PLANE, 512)
    edge_table = np.concatenate([both[..., 0:2], both[..., 18:20]], axis=-1).reshape(2, PLANE, 128)
    return ky_table, inner_table, edge_table


def body(coil_data, frame_of, basis, sample_pos, window_at, live_count):
    devices = 256
    data = coil_data.reshape(devices, 16, 2, LANES)
    coef = basis[frame_of.reshape(-1)].reshape(devices, 1, 2, 10)
    coef = jnp.pad(coef, ((0, 0), (0, 0), (0, 0), (0, LANES - 10)))
    sent = jnp.concatenate([data, coef], axis=1)
    got = lax.all_to_all(sent, ("kz", "tile"), split_axis=0, concat_axis=0, tiled=True)
    data = got[:, :16].reshape(2 * devices, 16, LANES)
    coef = got[:, 16, :, :10].astype(jnp.float32).reshape(-1)
    window = window_at.reshape(2 * devices, 2)
    live = (jnp.arange(2)[None, :] < live_count.reshape(devices, 1)).astype(jnp.float32).reshape(-1)
    pos = sample_pos.reshape(2 * devices, 2, LANES)
    inner, own, up, down = grid_tile(window[:, 0], window[:, 1], live, coef, pos, data)
    ky_table, inner_table, edge_table = [jnp.asarray(t) for t in make_tables()]
    return transform_plane(ky_table, inner_table, edge_table, inner, own, up, down)[None]


def solution(mesh):
    return jax.shard_map(
        body,
        mesh=mesh,
        in_specs=(
            P("kz", "tile", None, None, None, None, None),
            P("kz", "tile", None, None, None),
            P(),
            P("kz", "tile", None, None, None, None, None),
            P("kz", "tile", None, None, None, None),
            P("kz", "tile", None, None),
        ),
        out_specs=P("kz", None, "tile"),
        check_vma=False,
    )
```

time: 360 us -> 243 us (0.68); the launches traced: 353 us -> 242 us
  blocking collectives: 87.4 us -> 0 us
  Pallas kernels: 86.1 us -> 158 us
  waiting for transfers between devices: 87.4 us -> 55.2 us
  starting transfers between devices: 42.5 us -> 14.4 us
  local copies, waits for them, and re-layouts: 30.3 us -> 9.91 us
  other arithmetic: 19.5 us -> 4.98 us
    all_gather x1 -> x0, blocking collectives: 87.4 us -> none  [body(): lax.all_gather(frame_of.reshape(4, LANES), axes, axis=0, tiled=False)]
    pallas_call x5 -> x2, Pallas kernels: 86.1 us -> 158 us  [the longest x1 115 us: transform_plane(): pl.pallas_call(mid_kernel, out_shape=jax.ShapeDtypeStruct((PLANE, stages...]
    all_to_all x4 -> x1, starting transfers between devices: 40.5 us -> 14.4 us  [body(): lax.all_to_all(sent, ('kz', 'tile'), split_axis=0, concat_axis=0, tiled=T...]
    all_to_all x4 -> x1, waiting for transfers between devices: 81.1 us -> 55.2 us  [body(): lax.all_to_all(sent, ('kz', 'tile'), split_axis=0, concat_axis=0, tiled=T...]
    convert_element_type x3 -> x2, other arithmetic: 15.8 us -> 0.19 us  [the longest x1 0.1 us: body(): (jnp.arange(2)[None, :] < live_count.reshape(devices, 1)).astype(jnp.floa...]
    unnamed x35 -> x18, local copies, waits for them, and re-layouts: 18.4 us -> 6.27 us
    reshape x5 -> x2, local copies, waits for them, and re-layouts: 7.05 us -> 0.31 us  [the longest x1 0.17 us: body(): window = window_at.reshape(2 * devices, 2)]
    ppermute x2 -> x0, waiting for transfers between devices: 6.26 us -> none  [neighbour(): return lax.ppermute(value, 'tile', pairs)]
  transfers between devices with their start and end apart: 6 -> 1, of which waited for: 4 -> 1; matrix products, arithmetic and copies ran while one was open for 9% -> 0% of each run, Pallas kernels for 11% -> 0%
where the time goes in v2:
time: 243 us; the launch traced here: 242 us
  Pallas kernels  158 us (65%)
  waiting for transfers between devices  55.2 us (23%)
  starting transfers between devices  14.4 us (6%)
  local copies, waits for them, and re-layouts  9.91 us (4%)
  other arithmetic  4.98 us (2%)
    pallas_call x1, Pallas kernels, transform_plane(): pl.pallas_call(mid_kernel, out_shape=jax.ShapeDtypeStruct((PLANE, stages...  115 us
    all_to_all x1, waiting for transfers between devices, body(): lax.all_to_all(sent, ('kz', 'tile'), split_axis=0, concat_axis=0, tiled=T...  55.2 us
    pallas_call x1, Pallas kernels, grid_tile(): pl.pallas_call(functools.partial(grid_kernel, batch=batch), out_shape=[ja...  42.9 us
    all_to_all x1, starting transfers between devices, body(): lax.all_to_all(sent, ('kz', 'tile'), split_axis=0, concat_axis=0, tiled=T...  14.4 us
    unnamed x18, local copies, waits for them, and re-layouts  6.27 us
  transfers between devices with their start and end apart: 1, of which 1 were waited for; matrix products, arithmetic and copies ran while one was open for 0% of the time, Pallas kernels for 0%

profile of v2, /device:TPU:32, one launch (start us, length us, event | category | flops | bytes accessed | tf_op | source)
XLA Modules:
  0.0 242.3 jit_solution(275646345904620721)
XLA Ops:
  0.0 0.8 copy.18
  0.8 0.1 reshape.60
  1.0 1.0 copy.19
  2.0 1.3 gather_fusion
  3.3 4.8 %fusion = bf16[256,17,2,128]{3,2,1,0:T(2,128)(2,1)} fusion(bf16[256,1,2,10]{3,2,1,0:T(2,128)(2,1)S(1)} %bitcast.24, bf16[256,16,2,128]{3,2,1,0:T(2,128)(2,1)} %bitcast.23), kind=kLoop, calls=%fused_computation.2 | loop fusion | flops 6684672 | bytes 4335616 | tf_op jit(solution)/shard_map/concatenate | solution.py:339
  8.1 0.0 copy-start.6
  8.1 0.0 copy-start.5
  8.1 14.4 %all-to-all-start = ((bf16[256,17,2,128]{3,2,1,0:T(2,128)(2,1)}), bf16[256,17,2,128]{3,2,1,0:T(2,128)(2,1)S(1)}, u32[]{:S(2)}, u32[]{:S(2)}) async-start(bf16[256,17,2,128]{3,2,1,0:T(2,128)(2,1)} %fusion), calls=%async_computation | async-start | bytes 4456448 | tf_op jit(solution)/shard_map/all_to_all | solution.py:340
  22.5 0.0 copy-done.6
  22.5 0.1 lt.31
  22.6 0.1 fusion.1
  22.7 0.1 reshape.64.live_ref
  22.8 0.0 copy-done.5
  22.8 0.2 copy.17
  23.0 0.2 reshape.58
  23.2 55.2 %all-to-all-done = bf16[256,17,2,128]{3,2,1,0:T(2,128)(2,1)S(1)} async-done(((bf16[256,17,2,128]{3,2,1,0:T(2,128)(2,1)}), bf16[256,17,2,128]{3,2,1,0:T(2,128)(2,1)S(1)}, u32[]{:S(2)}, u32[]{:S(2)}) %all-to-all-start) | async-done | bytes 2228256 | tf_op jit(solution)/shard_map/all_to_all | solution.py:340
  78.4 0.1 slice_convert_fusion
  78.5 0.0 copy-start
  78.5 0.3 reshape.65.coef_ref
  78.9 1.4 slice.21
  80.3 0.0 copy-done
  80.3 0.0 copy-start.1
  80.3 0.0 copy-start.2
  80.3 0.0 copy-start.3
  80.3 42.9 %grid_tile.1 = (bf16[16,640,256]{2,1,0:T(8,128)(2,1)S(1)}, f32[4,640,256]{2,1,0:T(8,128)S(1)}, bf16[2,640,256]{2,1,0:T(8,128)(2,1)S(1)}, bf16[2,640,256]{2,1,0:T(8,128)(2,1)S(1)}) custom-call(s32[512]{0:T(512)S(1)} %bitcast.21, s32[512]{0:T(512)S(1)} %bitcast.20, f32[512]{0:T(512)S(1)} %reshape.64.live_ref, f32[5120]{0:T(1024)S(1)} %reshape.65.coef_ref, ...), custom_call_target="tpu_custom_call" | custom-call | flops 6000000000 | bytes 20971520 | tf_op jit(solution)/shard_map/grid_tile/pallas_call | solution.py:102
  123.2 0.0 copy-start.4
  123.2 2.3 copy-done.4
  125.5 0.0 copy-done.1
  125.5 0.0 copy-done.2
  125.5 0.0 copy-done.3
  125.5 114.7 %plane.1 = bf16[640,3200]{1,0:T(8,128)(2,1)S(1)} custom-call(bf16[5,128,1280]{2,1,0:T(8,128)(2,1)S(1)} %copy-done.1, bf16[2,640,512]{2,1,0:T(8,128)(2,1)S(1)} %copy-done.2, bf16[2,640,128]{2,1,0:T(8,128)(2,1)S(1)} %copy-done.3, bf16[16,640,256]{2,1,0:T(8,128)(2,1)} %copy-done.4, f32[4,640,256]{2,1,0:T(8,128)S(1)} %get-tuple-element.10.own_ref, ...), custom_call_target="tpu_custom_call" | custom-call | flops 20000000000 | bytes 20971520 | tf_op jit(solution)/shard_map/plane/pallas_call | solution.py:294
  240.3 2.0 copy.22
  (3 shorter events, 0.0 us)
Async XLA Ops:
  8.1 14.4 %copy-start.6 = (s32[1,1,8,32]{3,2,1,0:T(8,128)S(1)}, s32[1,1,8,32]{3,2,1,0:T(8,128)}, u32[]{:S(2)}) copy-start(s32[1,1,8,32]{3,2,1,0:T(8,128)} %param.14) | copy-start | bytes 3076
  8.1 14.7 %copy-start.5 = (s32[1,1,8,32,2,2]{3,5,4,2,1,0:T(2,128)S(1)}, s32[1,1,8,32,2,2]{3,5,4,2,1,0:T(2,128)}, u32[]{:S(2)}) copy-start(s32[1,1,8,32,2,2]{3,5,4,2,1,0:T(2,128)} %param.13) | copy-start | bytes 12292
  8.1 70.3 %all-to-all-start = ((bf16[256,17,2,128]{3,2,1,0:T(2,128)(2,1)}), bf16[256,17,2,128]{3,2,1,0:T(2,128)(2,1)S(1)}, u32[]{:S(2)}, u32[]{:S(2)}) async-start(bf16[256,17,2,128]{3,2,1,0:T(2,128)(2,1)} %fusion), calls=%async_computation | async-start | bytes 4456448 | tf_op jit(solution)/shard_map/all_to_all | solution.py:340
  78.5 1.8 copy-start
  80.3 45.2 %copy-start.1 = (bf16[5,128,1280]{2,1,0:T(8,128)(2,1)S(1)}, bf16[5,128,1280]{2,1,0:T(8,128)(2,1)}, u32[]{:S(2)}) copy-start(bf16[5,128,1280]{2,1,0:T(8,128)(2,1)} %constant.13.clone.ky_ref) | copy-start | bytes 4915204
  80.3 45.2 %copy-start.2 = (bf16[2,640,512]{2,1,0:T(8,128)(2,1)S(1)}, bf16[2,640,512]{2,1,0:T(8,128)(2,1)}, u32[]{:S(2)}) copy-start(bf16[2,640,512]{2,1,0:T(8,128)(2,1)} %constant.14.clone.inner_table_ref) | copy-start | bytes 3932164
  80.3 45.2 %copy-start.3 = (bf16[2,640,128]{2,1,0:T(8,128)(2,1)S(1)}, bf16[2,640,128]{2,1,0:T(8,128)(2,1)}, u32[]{:S(2)}) copy-start(bf16[2,640,128]{2,1,0:T(8,128)(2,1)} %constant.15.clone.edge_table_ref) | copy-start | bytes 983044
  123.2 2.3 copy-start.4

commit v3 on v2

--- a/solution.py
+++ b/solution.py
@@ -48,10 +48,12 @@
         scale = [coef_ref[s * 10 + r] for r in range(10)]
         re = jnp.concatenate([re * c for c in scale], axis=0).astype(jnp.bfloat16)
         im = jnp.concatenate([im * c for c in scale], axis=0).astype(jnp.bfloat16)
-        values = jnp.concatenate([re, zero, im, zero], axis=0)
-        return lax.dot_general(
-            weight, values, (((1,), (1,)), ((), ())), preferred_element_type=jnp.float32
-        )
+        re = jnp.concatenate([re, zero], axis=0)
+        im = jnp.concatenate([im, zero], axis=0)
+        across = (((1,), (1,)), ((), ()))
+        return [
+            lax.dot_general(weight, half, across, preferred_element_type=jnp.float32) for half in (re, im)
+        ]
 
     def step(b, carry):
         slots = [b * batch + k for k in range(batch)]
@@ -61,10 +63,86 @@
             start = pl.multiple_of(jnp.bitwise_and(col_ref[s], -8), 8)
             for i in range(WIN_ROWS):
                 at = (row + i, pl.ds(start, WIDE), slice(None))
-                acc_ref[at] += part[i * WIDE : (i + 1) * WIDE]
+                rows = slice(i * WIDE, (i + 1) * WIDE)
+                acc_ref[at] += jnp.concatenate([half[rows] for half in part], axis=1)
         return carry
 
     lax.fori_loop(0, count // batch, step, 0)
+
+
+def exchange_kernel(data_ref, coef_ref, data_out, coef_out,
+                    ready, data_send, data_recv, coef_send, coef_recv, own_sem):
+    parts, tiles = lax.axis_size("kz"), lax.axis_size("tile")
+    kz, tile = lax.axis_index("kz"), lax.axis_index("tile")
+    devices = parts * tiles
+    me = kz * tiles + tile
+    barrier = pltpu.get_barrier_semaphore()
+
+    def signal(sem, part, spot):
+        pl.semaphore_signal(sem, inc=1, device_id=(part, spot), device_id_type=pl.DeviceIdType.MESH)
+
+    def greet_tile(k, carry):
+        signal(barrier, kz, lax.rem(tile + k, tiles))
+        return carry
+
+    def greet_part(k, carry):
+        signal(barrier, lax.rem(kz + k, parts), tile)
+        return carry
+
+    def tell_part(k, carry):
+        signal(ready, lax.rem(kz + k, parts), tile)
+        return carry
+
+    lax.fori_loop(1, tiles, greet_tile, 0)
+    lax.fori_loop(1, parts, greet_part, 0)
+    pl.semaphore_wait(barrier, tiles + parts - 2)
+    lax.fori_loop(1, parts, tell_part, 0)
+    pl.semaphore_wait(ready, parts - 1)
+
+    def copies(source, k, target):
+        part = lax.rem(kz + k // tiles, parts)
+        spot = lax.rem(tile + lax.rem(k, tiles), tiles)
+        to = part * tiles + spot
+        pairs = ((data_ref, data_out, data_send, data_recv), (coef_ref, coef_out, coef_send, coef_recv))
+        return [
+            pltpu.make_async_remote_copy(
+                src_ref=src.at[source(to)], dst_ref=dst.at[target], send_sem=send, recv_sem=recv,
+                device_id=(part, spot), device_id_type=pl.DeviceIdType.MESH,
+            )
+            for src, dst, send, recv in pairs
+        ]
+
+    def send(k, carry):
+        for copy in copies(lambda to: to, k, me):
+            copy.start()
+        return carry
+
+    lax.fori_loop(1, devices, send, 0)
+    own = pltpu.make_async_copy(data_ref.at[me], data_out.at[me], own_sem)
+    own.start()
+    coef_out[me] = coef_ref[me]
+    own.wait()
+    others = pl.ds(0, devices - 1)
+    for copy in copies(lambda to: others, 1, others):
+        copy.wait_send()
+        copy.wait_recv()
+
+
+def exchange(data, coef):
+    dma = pltpu.SemaphoreType.DMA
+    return pl.pallas_call(
+        exchange_kernel,
+        out_shape=[
+            jax.ShapeDtypeStruct(data.shape, data.dtype),
+            jax.ShapeDtypeStruct(coef.shape, coef.dtype),
+        ],
+        in_specs=[ANY, VMEM],
+        out_specs=[ANY, VMEM],
+        scratch_shapes=[pltpu.SemaphoreType.REGULAR] + [dma] * 5,
+        compiler_params=pltpu.CompilerParams(collective_id=1, has_side_effects=True),
+        cost_estimate=pl.CostEstimate(flops=0, bytes_accessed=4 * MB, transcendentals=0),
+        name="exchange",
+    )(data, coef)
 
 
 def grid_kernel(row_ref, col_ref, live_ref, coef_ref, pos_ref, data_ref,
@@ -95,9 +173,10 @@
 
 SMEM = pl.BlockSpec(memory_space=pltpu.SMEM)
 VMEM = pl.BlockSpec(memory_space=pltpu.VMEM)
-
-
-def grid_tile(rows, cols, live, coef, pos, data, batch=4):
+ANY = pl.BlockSpec(memory_space=pl.ANY)
+
+
+def grid_tile(rows, cols, live, coef, pos, data, batch=32):
     wide = 2 * LANES
     return pl.pallas_call(
         functools.partial(grid_kernel, batch=batch),
@@ -311,7 +390,7 @@
             dma((2,)), dma((2,)), dma((stages,)), dma((stages,)), dma((stages,)), dma((stages,)),
         ],
         compiler_params=pltpu.CompilerParams(
-            vmem_limit_bytes=42 * MB, collective_id=0, has_side_effects=True
+            vmem_limit_bytes=36 * MB, collective_id=0, has_side_effects=True
         ),
         cost_estimate=pl.CostEstimate(flops=20 * 10**9, bytes_accessed=20 * MB, transcendentals=0),
         name="plane",
@@ -333,13 +412,11 @@
 
 def body(coil_data, frame_of, basis, sample_pos, window_at, live_count):
     devices = 256
-    data = coil_data.reshape(devices, 16, 2, LANES)
-    coef = basis[frame_of.reshape(-1)].reshape(devices, 1, 2, 10)
-    coef = jnp.pad(coef, ((0, 0), (0, 0), (0, 0), (0, LANES - 10)))
-    sent = jnp.concatenate([data, coef], axis=1)
-    got = lax.all_to_all(sent, ("kz", "tile"), split_axis=0, concat_axis=0, tiled=True)
-    data = got[:, :16].reshape(2 * devices, 16, LANES)
-    coef = got[:, 16, :, :10].astype(jnp.float32).reshape(-1)
+    coef = basis[frame_of.reshape(-1)].astype(jnp.float32).reshape(devices, 1, 20)
+    coef = jnp.pad(coef, ((0, 0), (0, 0), (0, LANES - 20)))
+    data, coef = exchange(coil_data.reshape(devices, 32, LANES), coef)
+    data = data.reshape(2 * devices, 16, LANES)
+    coef = coef[:, 0, :20].reshape(-1)
     window = window_at.reshape(2 * devices, 2)
     live = (jnp.arange(2)[None, :] < live_count.reshape(devices, 1)).astype(jnp.float32).reshape(-1)
     pos = sample_pos.reshape(2 * devices, 2, LANES)

time: 243 us -> 207 us (0.85)
  waiting for transfers between devices: 55.2 us -> 0 us
  Pallas kernels: 158 us -> 195 us
  starting transfers between devices: 14.4 us -> 0 us
  other arithmetic: 4.98 us -> 0.95 us
    pallas_call x0 -> x1, Pallas kernels: none -> 63.6 us  [exchange(): pl.pallas_call(exchange_kernel, out_shape=[jax.ShapeDtypeStruct(data.shap...]
    all_to_all x1 -> x0, waiting for transfers between devices: 55.2 us -> none  [body(): lax.all_to_all(sent, ('kz', 'tile'), split_axis=0, concat_axis=0, tiled=T...]
    pallas_call x1, Pallas kernels: 42.9 us -> 17.4 us  [grid_tile(): pl.pallas_call(functools.partial(grid_kernel, batch=batch), out_shape=[ja...]
    all_to_all x1 -> x0, starting transfers between devices: 14.4 us -> none  [body(): lax.all_to_all(sent, ('kz', 'tile'), split_axis=0, concat_axis=0, tiled=T...]
    concatenate x1 -> x0, other arithmetic: 4.78 us -> none  [body(): sent = jnp.concatenate([data, coef], axis=1)]
    unnamed x18 -> x14, local copies, waits for them, and re-layouts: 6.27 us -> 6.32 us
  transfers between devices with their start and end apart: 1 -> 0, of which waited for: 1 -> 0; matrix products, arithmetic and copies ran while one was open for 0% -> 0% of each run, Pallas kernels for 0% -> 0%
where the time goes in v3:
time: 207 us; the launch traced here: 206 us
  Pallas kernels  195 us (94%)
  local copies, waits for them, and re-layouts  10.4 us (5%)
    pallas_call x1, Pallas kernels, transform_plane(): pl.pallas_call(mid_kernel, out_shape=jax.ShapeDtypeStruct((PLANE, stages...  114 us
    pallas_call x1, Pallas kernels, exchange(): pl.pallas_call(exchange_kernel, out_shape=[jax.ShapeDtypeStruct(data.shap...  63.6 us
    pallas_call x1, Pallas kernels, grid_tile(): pl.pallas_call(functools.partial(grid_kernel, batch=batch), out_shape=[ja...  17.4 us
    unnamed x14, local copies, waits for them, and re-layouts  6.32 us

profile of v3, /device:TPU:32, one launch (start us, length us, event | category | flops | bytes accessed | tf_op | source)
XLA Modules:
  0.0 206.0 jit_solution(1639309636726203515)
XLA Ops:
  0.0 0.8 lt.31
  0.8 0.1 fusion
  0.9 0.1 reshape.69.live_ref
  1.0 0.8 copy.12
  1.8 0.1 reshape.66
  2.0 0.0 copy-start.1
  2.0 1.0 copy.13
  3.0 1.3 gather_fusion
  4.4 0.1 convert_element_type.24
  4.5 0.8 pad_convert_fusion.coef_ref
  5.3 0.9 copy.11
  6.2 0.2 reshape.64
  6.4 63.6 %exchange.1 = (bf16[256,32,128]{2,1,0:T(8,128)(2,1)}, f32[256,1,128]{2,1,0:T(1,128)}) custom-call(bf16[256,32,128]{2,1,0:T(8,128)(2,1)} %bitcast.20, f32[256,1,128]{2,1,0:T(1,128)} %pad_convert_fusion.coef_ref), custom_call_target="tpu_custom_call" | custom-call | bytes 4194304 | tf_op jit(solution)/shard_map/exchange/pallas_call | solution.py:133
  70.1 1.3 slice_reduce_fusion
  71.3 0.1 reshape_squeeze.3.coef_ref
  71.5 0.0 copy-done.1
  71.5 0.0 copy-start
  71.5 1.6 copy-done
  73.1 0.0 copy-start.2
  73.1 0.0 copy-start.3
  73.1 0.0 copy-start.4
  73.1 17.4 %grid_tile.1 = (bf16[16,640,256]{2,1,0:T(8,128)(2,1)S(1)}, f32[4,640,256]{2,1,0:T(8,128)S(1)}, bf16[2,640,256]{2,1,0:T(8,128)(2,1)S(1)}, bf16[2,640,256]{2,1,0:T(8,128)(2,1)S(1)}) custom-call(s32[512]{0:T(512)S(1)} %bitcast.17, s32[512]{0:T(512)S(1)} %bitcast.16, f32[512]{0:T(512)S(1)} %reshape.69.live_ref, f32[5120]{0:T(1024)S(1)} %reshape_squeeze.3.coef_ref, ...), custom_call_target="tpu_custom_call" | custom-call | flops 6000000000 | bytes 20971520 | tf_op jit(solution)/shard_map/grid_tile/pallas_call | solution.py:181
  90.5 0.0 copy-done.2
  90.5 0.0 copy-done.3
  90.5 0.0 copy-done.4
  90.5 113.5 %plane.1 = bf16[640,3200]{1,0:T(8,128)(2,1)S(1)} custom-call(bf16[5,128,1280]{2,1,0:T(8,128)(2,1)S(1)} %copy-done.2, bf16[2,640,512]{2,1,0:T(8,128)(2,1)S(1)} %copy-done.3, bf16[2,640,128]{2,1,0:T(8,128)(2,1)S(1)} %copy-done.4, bf16[16,640,256]{2,1,0:T(8,128)(2,1)S(1)} %get-tuple-element.13.grid_ref, f32[4,640,256]{2,1,0:T(8,128)S(1)} %get-tuple-element.14.own_ref, ...), custom_call_target="tpu_custom_call" | custom-call | flops 20000000000 | bytes 20971520 | tf_op jit(solution)/shard_map/plane/pallas_call | solution.py:373
  204.0 2.0 copy.16
  (3 shorter events, 0.0 us)
Async XLA Ops:
  2.0 69.5 %copy-start.1 = (f32[1,1,8,32,2,2,128]{6,5,4,3,2,1,0:T(2,128)S(1)}, f32[1,1,8,32,2,2,128]{6,5,4,3,2,1,0:T(2,128)}, u32[]{:S(2)}) copy-start(f32[1,1,8,32,2,2,128]{6,5,4,3,2,1,0:T(2,128)} %param.12) | copy-start | bytes 1572868
  71.5 1.6 copy-start
  73.1 17.4 %copy-start.2 = (bf16[5,128,1280]{2,1,0:T(8,128)(2,1)S(1)}, bf16[5,128,1280]{2,1,0:T(8,128)(2,1)}, u32[]{:S(2)}) copy-start(bf16[5,128,1280]{2,1,0:T(8,128)(2,1)} %constant.14.clone.ky_ref) | copy-start | bytes 4915204
  73.1 17.4 %copy-start.3 = (bf16[2,640,512]{2,1,0:T(8,128)(2,1)S(1)}, bf16[2,640,512]{2,1,0:T(8,128)(2,1)}, u32[]{:S(2)}) copy-start(bf16[2,640,512]{2,1,0:T(8,128)(2,1)} %constant.15.clone.inner_table_ref) | copy-start | bytes 3932164
  73.1 17.4 %copy-start.4 = (bf16[2,640,128]{2,1,0:T(8,128)(2,1)S(1)}, bf16[2,640,128]{2,1,0:T(8,128)(2,1)}, u32[]{:S(2)}) copy-start(bf16[2,640,128]{2,1,0:T(8,128)(2,1)} %constant.16.clone.edge_table_ref) | copy-start | bytes 983044

commit v4 on v2

--- a/solution.py
+++ b/solution.py
@@ -14,10 +14,10 @@
 WIN_ROWS = 4
 WIN_COLS = 32
 TILE_ROWS = 20
-WIDE = 40
-PAD = 680
+PAD = PLANE + WIN_COLS
 LANES = 128
 HALF = 80
+RANK = 10
 MB = 1024 * 1024
 
 
@@ -27,93 +27,183 @@
     return inner * inner
 
 
-def grid_slots(row_ref, col_ref, live_ref, coef_ref, pos_ref, data_ref, acc_ref, batch):
-    count = data_ref.shape[0]
-    row_cell = lax.broadcasted_iota(jnp.int32, (8, LANES), 0)
-    col_cell = lax.broadcasted_iota(jnp.int32, (WIDE, LANES), 0)
+SMEM = pl.BlockSpec(memory_space=pltpu.SMEM)
+VMEM = pl.BlockSpec(memory_space=pltpu.VMEM)
+HBM = pl.BlockSpec(memory_space=pltpu.HBM)
+
+
+def exchange_kernel(frame_ref, basis_ref, data_ref, data_out, coef_out,
+                    coef_ref, ready, data_send, data_recv, coef_send, coef_recv, own_sem):
+    parts, tiles = lax.axis_size("kz"), lax.axis_size("tile")
+    kz, tile = lax.axis_index("kz"), lax.axis_index("tile")
+    devices = parts * tiles
+    me = kz * tiles + tile
+    barrier = pltpu.get_barrier_semaphore()
+
+    def signal(sem, part, spot):
+        pl.semaphore_signal(sem, inc=1, device_id=(part, spot), device_id_type=pl.DeviceIdType.MESH)
+
+    def greet_tile(k, carry):
+        signal(barrier, kz, lax.rem(tile + k, tiles))
+        return carry
+
+    def greet_part(k, carry):
+        signal(barrier, lax.rem(kz + k, parts), tile)
+        return carry
+
+    def tell_part(k, carry):
+        signal(ready, lax.rem(kz + k, parts), tile)
+        return carry
+
+    lax.fori_loop(1, tiles, greet_tile, 0)
+    lax.fori_loop(1, parts, greet_part, 0)
+    pl.semaphore_wait(barrier, tiles + parts - 2)
+    lax.fori_loop(1, parts, tell_part, 0)
+    pl.semaphore_wait(ready, parts - 1)
+
+    def copies(pair, source, k, target):
+        part = lax.rem(kz + k // tiles, parts)
+        spot = lax.rem(tile + lax.rem(k, tiles), tiles)
+        src, dst, send, recv = pair
+        return pltpu.make_async_remote_copy(
+            src_ref=src.at[source(part * tiles + spot)], dst_ref=dst.at[target], send_sem=send, recv_sem=recv,
+            device_id=(part, spot), device_id_type=pl.DeviceIdType.MESH,
+        )
+
+    def send_all(pair):
+        def send(k, carry):
+            copies(pair, lambda to: to, k, me).start()
+            return carry
+
+        lax.fori_loop(1, devices, send, 0)
+
+    data = (data_ref, data_out, data_send, data_recv)
+    coef = (coef_ref, coef_out, coef_send, coef_recv)
+    send_all(data)
+    lane = lax.broadcasted_iota(jnp.int32, (1, 2 * RANK), 1)
+
+    def look_up(p, carry):
+        first, second = [basis_ref[pl.ds(frame_ref[p // tiles, s, lax.rem(p, tiles)], 1), :] for s in range(2)]
+        coef_ref[p] = jnp.where(lane < RANK, first, second)
+        return carry
+
+    lax.fori_loop(0, devices, look_up, 0, unroll=8)
+    send_all(coef)
+    own = pltpu.make_async_copy(data_ref.at[me], data_out.at[me], own_sem)
+    own.start()
+    coef_out[me] = coef_ref[me]
+    own.wait()
+    others = pl.ds(0, devices - 1)
+    for pair in (data, coef):
+        every = copies(pair, lambda to: others, 1, others)
+        every.wait_send()
+        every.wait_recv()
+
+
+def exchange(frames, table, data):
+    dma = pltpu.SemaphoreType.DMA
+    devices = data.shape[0]
+    return pl.pallas_call(
+        exchange_kernel,
+        out_shape=[
+            jax.ShapeDtypeStruct(data.shape, data.dtype),
+            jax.ShapeDtypeStruct((devices, 1, 2 * RANK), jnp.float32),
+        ],
+        in_specs=[SMEM, VMEM, HBM],
+        out_specs=[VMEM, VMEM],
+        scratch_shapes=[pltpu.VMEM((devices, 1, 2 * RANK), jnp.float32), pltpu.SemaphoreType.REGULAR] + [dma] * 5,
+        compiler_params=pltpu.CompilerParams(collective_id=1, has_side_effects=True, vmem_limit_bytes=8 * MB),
+        cost_estimate=pl.CostEstimate(flops=0, bytes_accessed=4 * MB, transcendentals=0),
+        name="exchange",
+    )(frames, table, data)
+
+
+def grid_slots(window_ref, live_ref, coef_ref, pos_ref, data_ref, acc_ref):
+    parts, slots, _, tiles = window_ref.shape
+    row_cell = lax.broadcasted_iota(jnp.int32, (8, LANES), 0).astype(jnp.float32)
+    col_cell = lax.broadcasted_iota(jnp.int32, (WIN_COLS, LANES), 0).astype(jnp.float32)
     zero = jnp.zeros((LANES - HALF, LANES), jnp.bfloat16)
 
-    def contribution(s):
-        col0 = col_ref[s]
-        shift = jnp.bitwise_and(col0, 7)
-        place = pos_ref[s]
-        u = place[0:1, :]
-        v = place[1:2, :]
-        row_k = taper(row_cell.astype(jnp.float32) - u) * live_ref[s]
-        col_k = taper((col_cell - shift).astype(jnp.float32) - v)
+    def contribution(a, t, s):
+        pair = a * tiles + t
+        place = pos_ref[pair * slots + s]
+        living = (s < live_ref[a, t]).astype(jnp.float32)
+        row_k = taper(row_cell - place[0:1, :]) * living
+        col_k = taper(col_cell - place[1:2, :])
         weight = jnp.concatenate([row_k[i : i + 1, :] * col_k for i in range(WIN_ROWS)], axis=0)
         weight = weight.astype(jnp.bfloat16)
-        data = data_ref[s].astype(jnp.float32)
-        re, im = data[0:8], data[8:16]
-        scale = [coef_ref[s * 10 + r] for r in range(10)]
-        re = jnp.concatenate([re * c for c in scale], axis=0).astype(jnp.bfloat16)
-        im = jnp.concatenate([im * c for c in scale], axis=0).astype(jnp.bfloat16)
-        values = jnp.concatenate([re, zero, im, zero], axis=0)
-        return lax.dot_general(
-            weight, values, (((1,), (1,)), ((), ())), preferred_element_type=jnp.float32
-        )
-
-    def step(b, carry):
-        slots = [b * batch + k for k in range(batch)]
-        parts = [contribution(s) for s in slots]
-        for s, part in zip(slots, parts):
-            row = row_ref[s] + 2
-            start = pl.multiple_of(jnp.bitwise_and(col_ref[s], -8), 8)
+        data = data_ref[pair, 16 * s : 16 * (s + 1)].astype(jnp.float32)
+        scale = [coef_ref[pair, 0, s * 10 + r] for r in range(10)]
+        across = (((1,), (1,)), ((), ()))
+        halves = []
+        for half in (data[0:8], data[8:16]):
+            values = jnp.concatenate([half * c for c in scale], axis=0).astype(jnp.bfloat16)
+            values = jnp.concatenate([values, zero], axis=0)
+            halves.append(lax.dot_general(weight, values, across, preferred_element_type=jnp.float32))
+        return halves
+
+    def step(a, carry):
+        slot_ids = [(t, s) for t in range(tiles) for s in range(slots)]
+        sums = [contribution(a, t, s) for t, s in slot_ids]
+        for (t, s), halves in zip(slot_ids, sums):
+            row = window_ref[a, s, 0, t] + 2
+            col = window_ref[a, s, 1, t]
             for i in range(WIN_ROWS):
-                at = (row + i, pl.ds(start, WIDE), slice(None))
-                acc_ref[at] += part[i * WIDE : (i + 1) * WIDE]
-        return carry
-
-    lax.fori_loop(0, count // batch, step, 0)
-
-
-def grid_kernel(row_ref, col_ref, live_ref, coef_ref, pos_ref, data_ref,
-                inner_ref, own_ref, up_ref, down_ref, acc_ref, *, batch):
+                for h, half in enumerate(halves):
+                    at = (h, row + i, pl.ds(col, WIN_COLS), slice(None))
+                    acc_ref[at] += half[i * WIN_COLS : (i + 1) * WIN_COLS]
+        return carry
+
+    lax.fori_loop(0, parts, step, 0)
+
+
+def grid_kernel(window_ref, live_ref, coef_ref, pos_ref, data_ref,
+                inner_ref, own_ref, up_ref, down_ref, acc_ref):
     def clear(k, carry):
-        acc_ref[k] = jnp.zeros(acc_ref.shape[1:], jnp.float32)
-        return carry
-
-    lax.fori_loop(0, acc_ref.shape[0], clear, 0)
-    grid_slots(row_ref, col_ref, live_ref, coef_ref, pos_ref, data_ref, acc_ref, batch)
-
-    def row_of(k):
-        wrap = acc_ref[k, 0:WIDE, :] + acc_ref[k, PLANE:PAD, :]
-        return jnp.concatenate([wrap, acc_ref[k, WIDE:PLANE, :]], axis=0)
+        for h in range(2):
+            acc_ref[h, k] = jnp.zeros(acc_ref.shape[2:], jnp.float32)
+        return carry
+
+    lax.fori_loop(0, acc_ref.shape[1], clear, 0)
+    grid_slots(window_ref, live_ref, coef_ref, pos_ref, data_ref, acc_ref)
+
+    def put(out_ref, k, row):
+        for h in range(2):
+            lanes = slice(h * LANES, (h + 1) * LANES)
+            wrap = acc_ref[h, row, 0:WIN_COLS, :] + acc_ref[h, row, PLANE:PAD, :]
+            out_ref[k, 0:WIN_COLS, lanes] = wrap.astype(out_ref.dtype)
+            out_ref[k, WIN_COLS:PLANE, lanes] = acc_ref[h, row, WIN_COLS:PLANE, :].astype(out_ref.dtype)
 
     for k in range(2):
-        up_ref[k] = row_of(k).astype(jnp.bfloat16)
-        down_ref[k] = row_of(TILE_ROWS + 2 + k).astype(jnp.bfloat16)
-        own_ref[k] = row_of(2 + k)
-        own_ref[2 + k] = row_of(TILE_ROWS + k)
+        put(up_ref, k, k)
+        put(down_ref, k, TILE_ROWS + 2 + k)
+        put(own_ref, k, 2 + k)
+        put(own_ref, 2 + k, TILE_ROWS + k)
 
     def emit(k, carry):
-        inner_ref[k] = row_of(k + 4).astype(jnp.bfloat16)
+        put(inner_ref, k, k + 4)
         return carry
 
     lax.fori_loop(0, TILE_ROWS - 4, emit, 0)
 
 
-SMEM = pl.BlockSpec(memory_space=pltpu.SMEM)
-VMEM = pl.BlockSpec(memory_space=pltpu.VMEM)
-
-
-def grid_tile(rows, cols, live, coef, pos, data, batch=4):
+def grid_tile(window, live, coef, pos, data):
     wide = 2 * LANES
     return pl.pallas_call(
-        functools.partial(grid_kernel, batch=batch),
+        grid_kernel,
         out_shape=[
             jax.ShapeDtypeStruct((TILE_ROWS - 4, PLANE, wide), jnp.bfloat16),
             jax.ShapeDtypeStruct((4, PLANE, wide), jnp.float32),
             jax.ShapeDtypeStruct((2, PLANE, wide), jnp.bfloat16),
             jax.ShapeDtypeStruct((2, PLANE, wide), jnp.bfloat16),
         ],
-        in_specs=[SMEM] * 4 + [VMEM] * 2,
+        in_specs=[SMEM] * 3 + [VMEM] * 2,
         out_specs=[VMEM] * 4,
-        scratch_shapes=[pltpu.VMEM((TILE_ROWS + 4, PAD, wide), jnp.float32)],
+        scratch_shapes=[pltpu.VMEM((2, TILE_ROWS + 4, PAD, LANES), jnp.float32)],
         compiler_params=pltpu.CompilerParams(vmem_limit_bytes=40 * MB),
         cost_estimate=pl.CostEstimate(flops=6 * 10**9, bytes_accessed=20 * MB, transcendentals=0),
         name="grid_tile",
-    )(rows, cols, live, coef, pos, data)
+    )(window, live, coef, pos, data)
 
 
 def interleave(pieces):
@@ -202,14 +292,14 @@
             rows_of(b, k, grid_ref, rot)
             return carry
 
-        lax.fori_loop(0, inner_rows, inner_row, 0)
+        lax.fori_loop(0, inner_rows, inner_row, 0, unroll=4)
 
         def inner_pack(d, carry):
             halves = [pieces_of(g * 8 * LANES + d * 4, 8) for g in range(2)]
             send_in[b, d] = jnp.concatenate(halves, axis=0).astype(jnp.bfloat16)
             return carry
 
-        lax.fori_loop(0, count, inner_pack, 0)
+        lax.fori_loop(0, count, inner_pack, 0, unroll=4)
         send_all(b, send_in, recv_in, send_sem_in, recv_sem_in)
 
         @pl.when(b == 0)
@@ -226,13 +316,13 @@
             rows_of(b, k, edge_grid, edge_rot)
             return carry
 
-        lax.fori_loop(0, 4, edge_row, 0)
+        lax.fori_loop(0, 4, edge_row, 0, unroll=4)
 
         def edge_pack(d, carry):
             send_ed[b, d] = pieces_of(d * 4, 4).astype(jnp.bfloat16)
             return carry
 
-        lax.fori_loop(0, count, edge_pack, 0)
+        lax.fori_loop(0, count, edge_pack, 0, unroll=4)
         send_all(b, send_ed, recv_ed, send_sem_ed, recv_sem_ed)
         return carry
 
@@ -311,7 +401,7 @@
             dma((2,)), dma((2,)), dma((stages,)), dma((stages,)), dma((stages,)), dma((stages,)),
         ],
         compiler_params=pltpu.CompilerParams(
-            vmem_limit_bytes=42 * MB, collective_id=0, has_side_effects=True
+            vmem_limit_bytes=36 * MB, collective_id=0, has_side_effects=True
         ),
         cost_estimate=pl.CostEstimate(flops=20 * 10**9, bytes_accessed=20 * MB, transcendentals=0),
         name="plane",
@@ -332,18 +422,14 @@
 
 
 def body(coil_data, frame_of, basis, sample_pos, window_at, live_count):
-    devices = 256
-    data = coil_data.reshape(devices, 16, 2, LANES)
-    coef = basis[frame_of.reshape(-1)].reshape(devices, 1, 2, 10)
-    coef = jnp.pad(coef, ((0, 0), (0, 0), (0, 0), (0, LANES - 10)))
-    sent = jnp.concatenate([data, coef], axis=1)
-    got = lax.all_to_all(sent, ("kz", "tile"), split_axis=0, concat_axis=0, tiled=True)
-    data = got[:, :16].reshape(2 * devices, 16, LANES)
-    coef = got[:, 16, :, :10].astype(jnp.float32).reshape(-1)
-    window = window_at.reshape(2 * devices, 2)
-    live = (jnp.arange(2)[None, :] < live_count.reshape(devices, 1)).astype(jnp.float32).reshape(-1)
-    pos = sample_pos.reshape(2 * devices, 2, LANES)
-    inner, own, up, down = grid_tile(window[:, 0], window[:, 1], live, coef, pos, data)
+    parts, tiles, slots, pair, samples = coil_data.shape[2:]
+    devices = parts * tiles
+    frames = frame_of[0, 0].transpose(0, 2, 1)
+    table = jnp.concatenate([basis, basis], axis=1).astype(jnp.float32)
+    data, coef = exchange(frames, table, coil_data.reshape(devices, slots * pair, samples))
+    window = window_at[0, 0].transpose(0, 2, 3, 1)
+    pos = sample_pos.reshape(devices * slots, 2, samples)
+    inner, own, up, down = grid_tile(window, live_count[0, 0], coef, pos, data)
     ky_table, inner_table, edge_table = [jnp.asarray(t) for t in make_tables()]
     return transform_plane(ky_table, inner_table, edge_table, inner, own, up, down)[None]
 

time: 243 us -> 201 us (0.83)
  waiting for transfers between devices: 55.2 us -> 0 us
  Pallas kernels: 158 us -> 195 us
  starting transfers between devices: 14.4 us -> 0 us
  local copies, waits for them, and re-layouts: 9.91 us -> 4.51 us
  other arithmetic: 4.98 us -> 0.85 us
    all_to_all x1 -> x0, waiting for transfers between devices: 55.2 us -> none  [body(): lax.all_to_all(sent, ('kz', 'tile'), split_axis=0, concat_axis=0, tiled=T...]
    pallas_call x1 -> x2, Pallas kernels: 42.9 us -> 82.2 us  [the longest x1 64.6 us: exchange(): pl.pallas_call(exchange_kernel, out_shape=[jax.ShapeDtypeStruct(data.shap...]
    all_to_all x1 -> x0, starting transfers between devices: 14.4 us -> none  [body(): lax.all_to_all(sent, ('kz', 'tile'), split_axis=0, concat_axis=0, tiled=T...]
    concatenate x1 -> x0, other arithmetic: 4.78 us -> none  [body(): sent = jnp.concatenate([data, coef], axis=1)]
    unnamed x18 -> x17, local copies, waits for them, and re-layouts: 6.27 us -> 4.3 us
  transfers between devices with their start and end apart: 1 -> 0, of which waited for: 1 -> 0; matrix products, arithmetic and copies ran while one was open for 0% -> 0% of each run, Pallas kernels for 0% -> 0%
where the time goes in v4:
time: 201 us; the launch traced here: 200 us
  Pallas kernels  195 us (97%)
  local copies, waits for them, and re-layouts  4.51 us (2%)
    pallas_call x1, Pallas kernels, transform_plane(): pl.pallas_call(mid_kernel, out_shape=jax.ShapeDtypeStruct((PLANE, stages...  113 us
    pallas_call x1, Pallas kernels, exchange(): pl.pallas_call(exchange_kernel, out_shape=[jax.ShapeDtypeStruct(data.shap...  64.6 us
    pallas_call x1, Pallas kernels, grid_tile(): pl.pallas_call(grid_kernel, out_shape=[jax.ShapeDtypeStruct((TILE_ROWS -...  17.6 us
    unnamed x17, local copies, waits for them, and re-layouts  4.3 us

profile of v4, /device:TPU:32, one launch (start us, length us, event | category | flops | bytes accessed | tf_op | source)
XLA Modules:
  0.0 200.2 jit_solution(6769047526685903345)
XLA Ops:
  0.0 0.0 copy-start.4
  0.0 0.0 copy-start.3
  0.0 0.0 copy-start.2
  0.0 0.9 maximum_convert_fusion
  0.9 0.2 copy.13.basis_ref
  1.1 0.0 copy-start
  1.1 1.6 copy-done
  2.7 0.0 copy-start.1
  2.7 0.7 copy-done.1
  3.4 64.6 %exchange.1 = (bf16[256,32,128]{2,1,0:T(8,128)(2,1)S(1)}, f32[256,1,20]{2,1,0:T(1,128)S(1)}) custom-call(s32[8,2,32]{2,1,0:T(2,128)S(1)} %bitcast.12, f32[1000,20]{1,0:T(8,128)S(1)} %copy.13.basis_ref, bf16[256,32,128]{2,1,0:T(8,128)(2,1)S(1)} %bitcast.11), custom_call_target="tpu_custom_call" | custom-call | bytes 4194304 | tf_op jit(solution)/shard_map/exchange/pallas_call | solution.py:106
  68.0 0.0 copy-done.4
  68.0 0.0 copy-done.3
  68.0 0.0 copy-done.2
  68.0 0.0 copy-start.5
  68.0 0.0 copy-start.6
  68.0 0.0 copy-start.7
  68.0 17.6 %grid_tile.1 = (bf16[16,640,256]{2,1,0:T(8,128)(2,1)S(1)}, f32[4,640,256]{2,1,0:T(8,128)S(1)}, bf16[2,640,256]{2,1,0:T(8,128)(2,1)S(1)}, bf16[2,640,256]{2,1,0:T(8,128)(2,1)S(1)}) custom-call(s32[8,2,2,32]{3,2,1,0:T(2,128)S(1)} %bitcast.14, s32[8,32]{1,0:T(8,128)S(1)} %bitcast.15, f32[256,1,20]{2,1,0:T(1,128)S(1)} %get-tuple-element.11.coef_ref, ...), custom_call_target="tpu_custom_call" | custom-call | flops 6000000000 | bytes 20971520 | tf_op jit(solution)/shard_map/grid_tile/pallas_call | solution.py:192
  85.7 0.0 copy-done.5
  85.7 0.0 copy-done.6
  85.7 0.0 copy-done.7
  85.7 112.5 %plane.1 = bf16[640,3200]{1,0:T(8,128)(2,1)S(1)} custom-call(bf16[5,128,1280]{2,1,0:T(8,128)(2,1)S(1)} %copy-done.5, bf16[2,640,512]{2,1,0:T(8,128)(2,1)S(1)} %copy-done.6, bf16[2,640,128]{2,1,0:T(8,128)(2,1)S(1)} %copy-done.7, bf16[16,640,256]{2,1,0:T(8,128)(2,1)S(1)} %get-tuple-element.13.grid_ref, f32[4,640,256]{2,1,0:T(8,128)S(1)} %get-tuple-element.14.own_ref, ...), custom_call_target="tpu_custom_call" | custom-call | flops 20000000000 | bytes 20971520 | tf_op jit(solution)/shard_map/plane/pallas_call | solution.py:384
  198.2 2.0 copy.15
Async XLA Ops:
  0.0 68.0 %copy-start.4 = (s32[1,1,8,32]{3,2,1,0:T(8,128)S(1)}, s32[1,1,8,32]{3,2,1,0:T(8,128)}, u32[]{:S(2)}) copy-start(s32[1,1,8,32]{3,2,1,0:T(8,128)} %param.14) | copy-start | bytes 3076
  0.0 68.0 %copy-start.3 = (s32[1,1,8,32,2,2]{3,5,4,2,1,0:T(2,128)S(1)}, s32[1,1,8,32,2,2]{3,5,4,2,1,0:T(2,128)}, u32[]{:S(2)}) copy-start(s32[1,1,8,32,2,2]{3,5,4,2,1,0:T(2,128)} %param.13) | copy-start | bytes 12292
  0.0 68.0 %copy-start.2 = (f32[1,1,8,32,2,2,128]{6,5,4,3,2,1,0:T(2,128)S(1)}, f32[1,1,8,32,2,2,128]{6,5,4,3,2,1,0:T(2,128)}, u32[]{:S(2)}) copy-start(f32[1,1,8,32,2,2,128]{6,5,4,3,2,1,0:T(2,128)} %param.12) | copy-start | bytes 1572868
  1.1 1.6 copy-start
  2.7 0.7 copy-start.1
  68.0 17.7 %copy-start.5 = (bf16[5,128,1280]{2,1,0:T(8,128)(2,1)S(1)}, bf16[5,128,1280]{2,1,0:T(8,128)(2,1)}, u32[]{:S(2)}) copy-start(bf16[5,128,1280]{2,1,0:T(8,128)(2,1)} %constant.6.clone.ky_ref) | copy-start | bytes 4915204
  68.0 17.7 %copy-start.6 = (bf16[2,640,512]{2,1,0:T(8,128)(2,1)S(1)}, bf16[2,640,512]{2,1,0:T(8,128)(2,1)}, u32[]{:S(2)}) copy-start(bf16[2,640,512]{2,1,0:T(8,128)(2,1)} %constant.7.clone.inner_table_ref) | copy-start | bytes 3932164
  68.0 17.7 %copy-start.7 = (bf16[2,640,128]{2,1,0:T(8,128)(2,1)S(1)}, bf16[2,640,128]{2,1,0:T(8,128)(2,1)}, u32[]{:S(2)}) copy-start(bf16[2,640,128]{2,1,0:T(8,128)(2,1)} %constant.8.clone.edge_table_ref) | copy-start | bytes 983044

commit v5 on v4

--- a/solution.py
+++ b/solution.py
@@ -17,6 +17,7 @@
 PAD = PLANE + WIN_COLS
 LANES = 128
 HALF = 80
+QUARTER = PLANE // 4
 RANK = 10
 MB = 1024 * 1024
 
@@ -167,16 +168,30 @@
     lax.fori_loop(0, acc_ref.shape[1], clear, 0)
     grid_slots(window_ref, live_ref, coef_ref, pos_ref, data_ref, acc_ref)
 
+    def fold(row, carry):
+        for h in range(2):
+            acc_ref[h, row, 0:WIN_COLS, :] += acc_ref[h, row, PLANE:PAD, :]
+        return carry
+
+    lax.fori_loop(0, acc_ref.shape[1], fold, 0)
+
     def put(out_ref, k, row):
         for h in range(2):
-            lanes = slice(h * LANES, (h + 1) * LANES)
-            wrap = acc_ref[h, row, 0:WIN_COLS, :] + acc_ref[h, row, PLANE:PAD, :]
-            out_ref[k, 0:WIN_COLS, lanes] = wrap.astype(out_ref.dtype)
-            out_ref[k, WIN_COLS:PLANE, lanes] = acc_ref[h, row, WIN_COLS:PLANE, :].astype(out_ref.dtype)
-
+            out_ref[k, :, h * LANES : (h + 1) * LANES] = acc_ref[h, row, 0:PLANE, :].astype(out_ref.dtype)
+
+    def put_dense(c, carry):
+        for out_ref, first in ((up_ref, 0), (down_ref, TILE_ROWS + 2)):
+            for k in range(2):
+                pieces = [
+                    acc_ref[h, first + k, pl.ds(pl.multiple_of(q * QUARTER + c * WIN_COLS, WIN_COLS), WIN_COLS), :]
+                    for q in range(4) for h in range(2)
+                ]
+                at = pl.ds(pl.multiple_of(c * WIN_COLS, WIN_COLS), WIN_COLS)
+                out_ref[k, at, :] = jnp.concatenate(interleave(pieces), axis=1).astype(jnp.bfloat16)
+        return carry
+
+    lax.fori_loop(0, QUARTER // WIN_COLS, put_dense, 0)
     for k in range(2):
-        put(up_ref, k, k)
-        put(down_ref, k, TILE_ROWS + 2 + k)
         put(own_ref, k, 2 + k)
         put(own_ref, 2 + k, TILE_ROWS + k)
 
@@ -194,8 +209,8 @@
         out_shape=[
             jax.ShapeDtypeStruct((TILE_ROWS - 4, PLANE, wide), jnp.bfloat16),
             jax.ShapeDtypeStruct((4, PLANE, wide), jnp.float32),
-            jax.ShapeDtypeStruct((2, PLANE, wide), jnp.bfloat16),
-            jax.ShapeDtypeStruct((2, PLANE, wide), jnp.bfloat16),
+            jax.ShapeDtypeStruct((2, QUARTER, PLANE), jnp.bfloat16),
+            jax.ShapeDtypeStruct((2, QUARTER, PLANE), jnp.bfloat16),
         ],
         in_specs=[SMEM] * 3 + [VMEM] * 2,
         out_specs=[VMEM] * 4,
@@ -218,6 +233,20 @@
     ]
 
 
+def separate(dense):
+    lane = lax.broadcasted_iota(jnp.int32, (dense.shape[0], LANES), 1)
+    pieces = []
+    for k in range(8):
+        tile, start = divmod(HALF * k, LANES)
+        piece = dense[:, tile * LANES : (tile + 1) * LANES]
+        if start + HALF > LANES:
+            piece = jnp.where(lane >= start, piece, dense[:, (tile + 1) * LANES : (tile + 2) * LANES])
+        if start:
+            piece = pltpu.roll(piece, LANES - start, 1)
+        pieces.append(jnp.where(lane < HALF, piece, 0.0))
+    return pieces
+
+
 def mid_kernel(ky_ref, inner_table_ref, edge_table_ref, grid_ref, own_ref, up_ref, down_ref, out_ref,
                send_in, send_ed, recv_in, recv_ed, halo, rot, edge_grid, edge_rot, re_ref, im_ref, edge_kx,
                halo_send, halo_recv, send_sem_in, recv_sem_in, send_sem_ed, recv_sem_ed):
@@ -306,9 +335,18 @@
         def _():
             to_below.wait()
             to_above.wait()
-            for k in range(2):
-                edge_grid[k] = (own_ref[k] + halo[0, k].astype(jnp.float32)).astype(jnp.bfloat16)
-                edge_grid[2 + k] = (own_ref[2 + k] + halo[1, k].astype(jnp.float32)).astype(jnp.bfloat16)
+
+            def add_halo(c, carry):
+                for k in range(4):
+                    at = pl.ds(pl.multiple_of(c * WIN_COLS, WIN_COLS), WIN_COLS)
+                    pieces = separate(halo[k // 2, k % 2, at, :].astype(jnp.float32))
+                    for p, piece in enumerate(pieces):
+                        cols = pl.ds(pl.multiple_of(p // 2 * QUARTER + c * WIN_COLS, WIN_COLS), WIN_COLS)
+                        lanes = slice(p % 2 * LANES, (p % 2 + 1) * LANES)
+                        edge_grid[k, cols, lanes] = (own_ref[k, cols, lanes] + piece).astype(jnp.bfloat16)
+                return carry
+
+            lax.fori_loop(0, QUARTER // WIN_COLS, add_halo, 0)
             for k in range(4):
                 edge_rot[k] = turned(edge_grid[k])
 
@@ -391,7 +429,7 @@
             pltpu.VMEM((stages, count, 4, PLANE), bf16),
             pltpu.VMEM((stages, count, rows, PLANE), bf16),
             pltpu.VMEM((stages, count, 4, PLANE), bf16),
-            pltpu.VMEM((2, 2, PLANE, wide), bf16),
+            pltpu.VMEM((2, 2, QUARTER, PLANE), bf16),
             pltpu.VMEM((rows, PLANE, wide), bf16),
             pltpu.VMEM((4, PLANE, wide), bf16),
             pltpu.VMEM((4, PLANE, wide), bf16),

time: 201 us -> 197 us (0.980)
  Pallas kernels: 195 us -> 191 us
    pallas_call x1, Pallas kernels: 113 us -> 108 us  [transform_plane(): pl.pallas_call(mid_kernel, out_shape=jax.ShapeDtypeStruct((PLANE, stages...]
where the time goes in v5:
time: 197 us; the launch traced here: 196 us
  Pallas kernels  191 us (97%)
  local copies, waits for them, and re-layouts  4.51 us (2%)
    pallas_call x1, Pallas kernels, transform_plane(): pl.pallas_call(mid_kernel, out_shape=jax.ShapeDtypeStruct((PLANE, stages...  108 us
    pallas_call x1, Pallas kernels, exchange(): pl.pallas_call(exchange_kernel, out_shape=[jax.ShapeDtypeStruct(data.shap...  64.6 us
    pallas_call x1, Pallas kernels, grid_tile(): pl.pallas_call(grid_kernel, out_shape=[jax.ShapeDtypeStruct((TILE_ROWS -...  18.7 us
    unnamed x17, local copies, waits for them, and re-layouts  4.3 us

profile of v5, /device:TPU:32, one launch (start us, length us, event | category | flops | bytes accessed | tf_op | source)
XLA Modules:
  0.0 196.4 jit_solution(12753365193279021533)
XLA Ops:
  0.0 0.0 copy-start.4
  0.0 0.0 copy-start.3
  0.0 0.0 copy-start.2
  0.0 0.9 maximum_convert_fusion
  0.9 0.2 copy.13.basis_ref
  1.1 0.0 copy-start
  1.1 1.6 copy-done
  2.7 0.0 copy-start.1
  2.7 0.7 copy-done.1
  3.4 64.6 %exchange.1 = (bf16[256,32,128]{2,1,0:T(8,128)(2,1)S(1)}, f32[256,1,20]{2,1,0:T(1,128)S(1)}) custom-call(s32[8,2,32]{2,1,0:T(2,128)S(1)} %bitcast.12, f32[1000,20]{1,0:T(8,128)S(1)} %copy.13.basis_ref, bf16[256,32,128]{2,1,0:T(8,128)(2,1)S(1)} %bitcast.11), custom_call_target="tpu_custom_call" | custom-call | bytes 4194304 | tf_op jit(solution)/shard_map/exchange/pallas_call | solution.py:107
  68.0 0.0 copy-done.4
  68.0 0.0 copy-done.3
  68.0 0.0 copy-done.2
  68.0 0.0 copy-start.5
  68.0 0.0 copy-start.6
  68.0 0.0 copy-start.7
  68.0 18.7 %grid_tile.1 = (bf16[16,640,256]{2,1,0:T(8,128)(2,1)S(1)}, f32[4,640,256]{2,1,0:T(8,128)S(1)}, bf16[2,160,640]{2,1,0:T(8,128)(2,1)S(1)}, bf16[2,160,640]{2,1,0:T(8,128)(2,1)S(1)}) custom-call(s32[8,2,2,32]{3,2,1,0:T(2,128)S(1)} %bitcast.14, s32[8,32]{1,0:T(8,128)S(1)} %bitcast.15, f32[256,1,20]{2,1,0:T(1,128)S(1)} %get-tuple-element.11.coef_ref, ...), custom_call_target="tpu_custom_call" | custom-call | flops 6000000000 | bytes 20971520 | tf_op jit(solution)/shard_map/grid_tile/pallas_call | solution.py:207
  86.7 0.0 copy-done.5
  86.8 0.0 copy-done.6
  86.8 0.0 copy-done.7
  86.8 107.6 %plane.1 = bf16[640,3200]{1,0:T(8,128)(2,1)S(1)} custom-call(bf16[5,128,1280]{2,1,0:T(8,128)(2,1)S(1)} %copy-done.5, bf16[2,640,512]{2,1,0:T(8,128)(2,1)S(1)} %copy-done.6, bf16[2,640,128]{2,1,0:T(8,128)(2,1)S(1)} %copy-done.7, bf16[16,640,256]{2,1,0:T(8,128)(2,1)S(1)} %get-tuple-element.13.grid_ref, f32[4,640,256]{2,1,0:T(8,128)S(1)} %get-tuple-element.14.own_ref, ...), custom_call_target="tpu_custom_call" | custom-call | flops 20000000000 | bytes 20971520 | tf_op jit(solution)/shard_map/plane/pallas_call | solution.py:422
  194.4 2.0 %copy.15 = bf16[1,640,3200]{2,1,0:T(8,128)(2,1)} copy(bf16[1,640,3200]{2,1,0:T(8,128)(2,1)S(1)} %bitcast.10) | data formatting | bytes 8192000
Async XLA Ops:
  0.0 68.0 %copy-start.4 = (s32[1,1,8,32]{3,2,1,0:T(8,128)S(1)}, s32[1,1,8,32]{3,2,1,0:T(8,128)}, u32[]{:S(2)}) copy-start(s32[1,1,8,32]{3,2,1,0:T(8,128)} %param.14) | copy-start | bytes 3076
  0.0 68.0 %copy-start.3 = (s32[1,1,8,32,2,2]{3,5,4,2,1,0:T(2,128)S(1)}, s32[1,1,8,32,2,2]{3,5,4,2,1,0:T(2,128)}, u32[]{:S(2)}) copy-start(s32[1,1,8,32,2,2]{3,5,4,2,1,0:T(2,128)} %param.13) | copy-start | bytes 12292
  0.0 68.0 %copy-start.2 = (f32[1,1,8,32,2,2,128]{6,5,4,3,2,1,0:T(2,128)S(1)}, f32[1,1,8,32,2,2,128]{6,5,4,3,2,1,0:T(2,128)}, u32[]{:S(2)}) copy-start(f32[1,1,8,32,2,2,128]{6,5,4,3,2,1,0:T(2,128)} %param.12) | copy-start | bytes 1572868
  1.1 1.6 copy-start
  2.7 0.7 copy-start.1
  68.0 18.8 %copy-start.5 = (bf16[5,128,1280]{2,1,0:T(8,128)(2,1)S(1)}, bf16[5,128,1280]{2,1,0:T(8,128)(2,1)}, u32[]{:S(2)}) copy-start(bf16[5,128,1280]{2,1,0:T(8,128)(2,1)} %constant.6.clone.ky_ref) | copy-start | bytes 4915204
  68.0 18.8 %copy-start.6 = (bf16[2,640,512]{2,1,0:T(8,128)(2,1)S(1)}, bf16[2,640,512]{2,1,0:T(8,128)(2,1)}, u32[]{:S(2)}) copy-start(bf16[2,640,512]{2,1,0:T(8,128)(2,1)} %constant.7.clone.inner_table_ref) | copy-start | bytes 3932164
  68.0 18.8 %copy-start.7 = (bf16[2,640,128]{2,1,0:T(8,128)(2,1)S(1)}, bf16[2,640,128]{2,1,0:T(8,128)(2,1)}, u32[]{:S(2)}) copy-start(bf16[2,640,128]{2,1,0:T(8,128)(2,1)} %constant.8.clone.edge_table_ref) | copy-start | bytes 983044

commit v6 on v5

--- a/solution.py
+++ b/solution.py
@@ -19,6 +19,7 @@
 HALF = 80
 QUARTER = PLANE // 4
 RANK = 10
+DEPTH = 8
 MB = 1024 * 1024
 
 
@@ -33,8 +34,8 @@
 HBM = pl.BlockSpec(memory_space=pltpu.HBM)
 
 
-def exchange_kernel(frame_ref, basis_ref, data_ref, data_out, coef_out,
-                    coef_ref, ready, data_send, data_recv, coef_send, coef_recv, own_sem):
+def exchange_kernel(frame_ref, data_ref, data_out, frame_out, spread, met, total,
+                    ready, data_send, data_recv, met_send, met_recv, frame_send, frame_recv, own_sem):
     parts, tiles = lax.axis_size("kz"), lax.axis_size("tile")
     kz, tile = lax.axis_index("kz"), lax.axis_index("tile")
     devices = parts * tiles
@@ -62,64 +63,100 @@
     lax.fori_loop(1, parts, tell_part, 0)
     pl.semaphore_wait(ready, parts - 1)
 
-    def copies(pair, source, k, target):
+    def copy_to(part, spot, src, dst, send, recv):
+        return pltpu.make_async_remote_copy(
+            src_ref=src, dst_ref=dst, send_sem=send, recv_sem=recv,
+            device_id=(part, spot), device_id_type=pl.DeviceIdType.MESH,
+        )
+
+    def send_data(k, carry):
         part = lax.rem(kz + k // tiles, parts)
         spot = lax.rem(tile + lax.rem(k, tiles), tiles)
-        src, dst, send, recv = pair
-        return pltpu.make_async_remote_copy(
-            src_ref=src.at[source(part * tiles + spot)], dst_ref=dst.at[target], send_sem=send, recv_sem=recv,
-            device_id=(part, spot), device_id_type=pl.DeviceIdType.MESH,
-        )
-
-    def send_all(pair):
-        def send(k, carry):
-            copies(pair, lambda to: to, k, me).start()
-            return carry
-
-        lax.fori_loop(1, devices, send, 0)
-
-    data = (data_ref, data_out, data_send, data_recv)
-    coef = (coef_ref, coef_out, coef_send, coef_recv)
-    send_all(data)
-    lane = lax.broadcasted_iota(jnp.int32, (1, 2 * RANK), 1)
-
-    def look_up(p, carry):
-        first, second = [basis_ref[pl.ds(frame_ref[p // tiles, s, lax.rem(p, tiles)], 1), :] for s in range(2)]
-        coef_ref[p] = jnp.where(lane < RANK, first, second)
-        return carry
-
-    lax.fori_loop(0, devices, look_up, 0, unroll=8)
-    send_all(coef)
+        to = part * tiles + spot
+        copy_to(part, spot, data_ref.at[to], data_out.at[me], data_send, data_recv).start()
+        return carry
+
+    lax.fori_loop(1, tiles, send_data, 0)
+
+    columns = tiles // DEPTH
+    groups = parts * columns
+    column, level = tile // DEPTH, lax.rem(tile, DEPTH)
+    mine = kz * columns + column
+    lane = lax.broadcasted_iota(jnp.int32, (1, LANES), 1)
+
+    def place(d, carry):
+        first, second = [frame_ref[d // tiles, s, lax.rem(d, tiles)] for s in range(2)]
+        spread[d] = jnp.where(lane == 2 * mine, first, jnp.where(lane == 2 * mine + 1, second, 0))
+        return carry
+
+    lax.fori_loop(0, devices, place, 0, unroll=8)
+
+    def send_met(k, carry):
+        group = lax.rem(mine + k, groups)
+        part, spot = group // columns, lax.rem(group, columns) * DEPTH + level
+        levels = pl.ds(group * DEPTH, DEPTH)
+        copy_to(part, spot, spread.at[levels], met.at[mine], met_send, met_recv).start()
+        return carry
+
+    lax.fori_loop(1, groups, send_met, 0)
+    lax.fori_loop(tiles, devices, send_data, 0)
     own = pltpu.make_async_copy(data_ref.at[me], data_out.at[me], own_sem)
     own.start()
-    coef_out[me] = coef_ref[me]
+    met[mine] = spread[pl.ds(mine * DEPTH, DEPTH)]
+    others = pl.ds(0, groups - 1)
+    rows = pl.ds(0, (groups - 1) * DEPTH)
+    copy_to(kz, lax.rem(tile + 1, tiles), spread.at[rows], spread.at[rows], met_send, met_recv).wait_send()
+    copy_to(kz, lax.rem(tile + 1, tiles), met.at[others], met.at[others], met_send, met_recv).wait_recv()
+
+    def add(g, carry):
+        return carry + met[g]
+
+    total[...] = lax.fori_loop(0, groups, add, jnp.zeros(total.shape, jnp.int32))
+
+    def send_frames(k, carry):
+        to = lax.rem(level + k, DEPTH)
+        copy_to(kz, column * DEPTH + to, total.at[to], frame_out.at[level], frame_send, frame_recv).start()
+        return carry
+
+    lax.fori_loop(1, DEPTH, send_frames, 0)
+    frame_out[level] = total[level]
     own.wait()
     others = pl.ds(0, devices - 1)
-    for pair in (data, coef):
-        every = copies(pair, lambda to: others, 1, others)
+    levels = pl.ds(0, DEPTH - 1)
+    beside = (kz, lax.rem(tile + 1, tiles))
+    for every in (
+        copy_to(*beside, data_ref.at[others], data_out.at[others], data_send, data_recv),
+        copy_to(*beside, total.at[levels], frame_out.at[levels], frame_send, frame_recv),
+    ):
         every.wait_send()
         every.wait_recv()
 
 
-def exchange(frames, table, data):
+def exchange(frames, data):
     dma = pltpu.SemaphoreType.DMA
     devices = data.shape[0]
+    groups = devices // DEPTH
     return pl.pallas_call(
         exchange_kernel,
         out_shape=[
             jax.ShapeDtypeStruct(data.shape, data.dtype),
-            jax.ShapeDtypeStruct((devices, 1, 2 * RANK), jnp.float32),
+            jax.ShapeDtypeStruct((DEPTH, 1, LANES), jnp.int32),
         ],
-        in_specs=[SMEM, VMEM, HBM],
+        in_specs=[SMEM, HBM],
         out_specs=[VMEM, VMEM],
-        scratch_shapes=[pltpu.VMEM((devices, 1, 2 * RANK), jnp.float32), pltpu.SemaphoreType.REGULAR] + [dma] * 5,
-        compiler_params=pltpu.CompilerParams(collective_id=1, has_side_effects=True, vmem_limit_bytes=8 * MB),
+        scratch_shapes=[
+            pltpu.VMEM((devices, 1, LANES), jnp.int32),
+            pltpu.VMEM((groups, DEPTH, 1, LANES), jnp.int32),
+            pltpu.VMEM((DEPTH, 1, LANES), jnp.int32),
+            pltpu.SemaphoreType.REGULAR,
+        ] + [dma] * 7,
+        compiler_params=pltpu.CompilerParams(collective_id=1, has_side_effects=True, vmem_limit_bytes=50 * MB),
         cost_estimate=pl.CostEstimate(flops=0, bytes_accessed=4 * MB, transcendentals=0),
         name="exchange",
-    )(frames, table, data)
-
-
-def grid_slots(window_ref, live_ref, coef_ref, pos_ref, data_ref, acc_ref):
+    )(frames, data)
+
+
+def grid_slots(window_ref, live_ref, frame_ref, basis_ref, pos_ref, data_ref, acc_ref):
     parts, slots, _, tiles = window_ref.shape
     row_cell = lax.broadcasted_iota(jnp.int32, (8, LANES), 0).astype(jnp.float32)
     col_cell = lax.broadcasted_iota(jnp.int32, (WIN_COLS, LANES), 0).astype(jnp.float32)
@@ -134,7 +171,8 @@
         weight = jnp.concatenate([row_k[i : i + 1, :] * col_k for i in range(WIN_ROWS)], axis=0)
         weight = weight.astype(jnp.bfloat16)
         data = data_ref[pair, 16 * s : 16 * (s + 1)].astype(jnp.float32)
-        scale = [coef_ref[pair, 0, s * 10 + r] for r in range(10)]
+        frame = frame_ref[t % DEPTH, 0, 2 * (a * (tiles // DEPTH) + t // DEPTH) + s]
+        scale = [basis_ref[r, frame] for r in range(RANK)]
         across = (((1,), (1,)), ((), ()))
         halves = []
         for half in (data[0:8], data[8:16]):
@@ -158,7 +196,7 @@
     lax.fori_loop(0, parts, step, 0)
 
 
-def grid_kernel(window_ref, live_ref, coef_ref, pos_ref, data_ref,
+def grid_kernel(window_ref, live_ref, frame_ref, basis_ref, pos_ref, data_ref,
                 inner_ref, own_ref, up_ref, down_ref, acc_ref):
     def clear(k, carry):
         for h in range(2):
@@ -166,7 +204,7 @@
         return carry
 
     lax.fori_loop(0, acc_ref.shape[1], clear, 0)
-    grid_slots(window_ref, live_ref, coef_ref, pos_ref, data_ref, acc_ref)
+    grid_slots(window_ref, live_ref, frame_ref, basis_ref, pos_ref, data_ref, acc_ref)
 
     def fold(row, carry):
         for h in range(2):
@@ -202,7 +240,7 @@
     lax.fori_loop(0, TILE_ROWS - 4, emit, 0)
 
 
-def grid_tile(window, live, coef, pos, data):
+def grid_tile(window, live, frames, basis, pos, data):
     wide = 2 * LANES
     return pl.pallas_call(
         grid_kernel,
@@ -212,13 +250,13 @@
             jax.ShapeDtypeStruct((2, QUARTER, PLANE), jnp.bfloat16),
             jax.ShapeDtypeStruct((2, QUARTER, PLANE), jnp.bfloat16),
         ],
-        in_specs=[SMEM] * 3 + [VMEM] * 2,
+        in_specs=[SMEM] * 4 + [VMEM] * 2,
         out_specs=[VMEM] * 4,
         scratch_shapes=[pltpu.VMEM((2, TILE_ROWS + 4, PAD, LANES), jnp.float32)],
         compiler_params=pltpu.CompilerParams(vmem_limit_bytes=40 * MB),
         cost_estimate=pl.CostEstimate(flops=6 * 10**9, bytes_accessed=20 * MB, transcendentals=0),
         name="grid_tile",
-    )(window, live, coef, pos, data)
+    )(window, live, frames, basis, pos, data)
 
 
 def interleave(pieces):
@@ -463,11 +501,11 @@
     parts, tiles, slots, pair, samples = coil_data.shape[2:]
     devices = parts * tiles
     frames = frame_of[0, 0].transpose(0, 2, 1)
-    table = jnp.concatenate([basis, basis], axis=1).astype(jnp.float32)
-    data, coef = exchange(frames, table, coil_data.reshape(devices, slots * pair, samples))
+    table = basis.T.astype(jnp.float32)
+    data, frames = exchange(frames, coil_data.reshape(devices, slots * pair, samples))
     window = window_at[0, 0].transpose(0, 2, 3, 1)
     pos = sample_pos.reshape(devices * slots, 2, samples)
-    inner, own, up, down = grid_tile(window, live_count[0, 0], coef, pos, data)
+    inner, own, up, down = grid_tile(window, live_count[0, 0], frames, table, pos, data)
     ky_table, inner_table, edge_table = [jnp.asarray(t) for t in make_tables()]
     return transform_plane(ky_table, inner_table, edge_table, inner, own, up, down)[None]
 

time: 197 us -> 193 us (0.980)
  Pallas kernels: 191 us -> 186 us
    pallas_call x1, Pallas kernels: 64.6 us -> 60.6 us  [exchange(): pl.pallas_call(exchange_kernel, out_shape=[jax.ShapeDtypeStruct(data.shap...]
    unnamed x17 -> x15, local copies, waits for them, and re-layouts: 4.3 us -> 5.13 us
where the time goes in v6:
time: 193 us; the launch traced here: 192 us
  Pallas kernels  186 us (96%)
  local copies, waits for them, and re-layouts  5.13 us (3%)
    pallas_call x1, Pallas kernels, transform_plane(): pl.pallas_call(mid_kernel, out_shape=jax.ShapeDtypeStruct((PLANE, stages...  108 us
    pallas_call x1, Pallas kernels, exchange(): pl.pallas_call(exchange_kernel, out_shape=[jax.ShapeDtypeStruct(data.shap...  60.6 us
    pallas_call x1, Pallas kernels, grid_tile(): pl.pallas_call(grid_kernel, out_shape=[jax.ShapeDtypeStruct((TILE_ROWS -...  17.5 us
    unnamed x15, local copies, waits for them, and re-layouts  5.13 us

profile of v6, /device:TPU:32, one launch (start us, length us, event | category | flops | bytes accessed | tf_op | source)
XLA Modules:
  0.0 192.2 jit_solution(1078145998769539061)
XLA Ops:
  0.0 0.8 convert_bitcast_fusion.basis_ref
  0.8 0.0 copy-start
  0.8 0.7 copy-done
  1.5 60.6 %exchange.1 = (bf16[256,32,128]{2,1,0:T(8,128)(2,1)S(1)}, s32[8,1,128]{2,1,0:T(1,128)S(1)}) custom-call(s32[8,2,32]{2,1,0:T(2,128)S(1)} %bitcast.13, bf16[256,32,128]{2,1,0:T(8,128)(2,1)} %bitcast.17), custom_call_target="tpu_custom_call" | custom-call | bytes 4194304 | tf_op jit(solution)/shard_map/exchange/pallas_call | solution.py:139
  62.0 0.0 copy-start.1
  62.1 1.0 copy-done.1
  63.1 0.0 copy-start.2
  63.1 0.7 copy-done.2
  63.8 0.0 copy-start.3
  63.8 0.7 copy-done.3
  64.5 0.0 copy-start.4
  64.5 0.0 copy-start.5
  64.5 0.0 copy-start.6
  64.5 17.5 %grid_tile.1 = (bf16[16,640,256]{2,1,0:T(8,128)(2,1)S(1)}, f32[4,640,256]{2,1,0:T(8,128)S(1)}, bf16[2,160,640]{2,1,0:T(8,128)(2,1)S(1)}, bf16[2,160,640]{2,1,0:T(8,128)(2,1)S(1)}) custom-call(s32[8,2,2,32]{3,2,1,0:T(2,128)S(1)} %bitcast.15, s32[8,32]{1,0:T(8,128)S(1)} %bitcast.16, s32[8,1,128]{2,1,0:T(1,128)S(1)} %get-tuple-element.11.frame_ref, ...), custom_call_target="tpu_custom_call" | custom-call | flops 6000000000 | bytes 20971520 | tf_op jit(solution)/shard_map/grid_tile/pallas_call | solution.py:245
  82.0 0.0 copy-done.4
  82.0 0.0 copy-done.5
  82.0 0.0 copy-done.6
  82.0 108.2 %plane.1 = bf16[640,3200]{1,0:T(8,128)(2,1)S(1)} custom-call(bf16[5,128,1280]{2,1,0:T(8,128)(2,1)S(1)} %copy-done.4, bf16[2,640,512]{2,1,0:T(8,128)(2,1)S(1)} %copy-done.5, bf16[2,640,128]{2,1,0:T(8,128)(2,1)S(1)} %copy-done.6, bf16[16,640,256]{2,1,0:T(8,128)(2,1)S(1)} %get-tuple-element.13.grid_ref, f32[4,640,256]{2,1,0:T(8,128)S(1)} %get-tuple-element.14.own_ref, ...), custom_call_target="tpu_custom_call" | custom-call | flops 20000000000 | bytes 20971520 | tf_op jit(solution)/shard_map/plane/pallas_call | solution.py:460
  190.2 2.0 %copy.11 = bf16[1,640,3200]{2,1,0:T(8,128)(2,1)} copy(bf16[1,640,3200]{2,1,0:T(8,128)(2,1)S(1)} %bitcast.12) | data formatting | bytes 8192000
Async XLA Ops:
  0.8 0.7 copy-start
  62.0 1.0 copy-start.1
  63.1 0.7 copy-start.2
  63.8 0.7 copy-start.3
  64.5 17.5 %copy-start.4 = (bf16[5,128,1280]{2,1,0:T(8,128)(2,1)S(1)}, bf16[5,128,1280]{2,1,0:T(8,128)(2,1)}, u32[]{:S(2)}) copy-start(bf16[5,128,1280]{2,1,0:T(8,128)(2,1)} %constant.6.clone.ky_ref) | copy-start | bytes 4915204
  64.5 17.5 %copy-start.5 = (bf16[2,640,512]{2,1,0:T(8,128)(2,1)S(1)}, bf16[2,640,512]{2,1,0:T(8,128)(2,1)}, u32[]{:S(2)}) copy-start(bf16[2,640,512]{2,1,0:T(8,128)(2,1)} %constant.7.clone.inner_table_ref) | copy-start | bytes 3932164
  64.5 17.5 %copy-start.6 = (bf16[2,640,128]{2,1,0:T(8,128)(2,1)S(1)}, bf16[2,640,128]{2,1,0:T(8,128)(2,1)}, u32[]{:S(2)}) copy-start(bf16[2,640,128]{2,1,0:T(8,128)(2,1)} %constant.8.clone.edge_table_ref) | copy-start | bytes 983044

commit v7 on v6

--- a/solution.py
+++ b/solution.py
@@ -34,7 +34,7 @@
 HBM = pl.BlockSpec(memory_space=pltpu.HBM)
 
 
-def exchange_kernel(frame_ref, data_ref, data_out, frame_out, spread, met, total,
+def exchange_kernel(frame_ref, basis_ref, data_ref, data_out, frame_out, basis_out, sums_out, spread, met, total,
                     ready, data_send, data_recv, met_send, met_recv, frame_send, frame_recv, own_sem):
     parts, tiles = lax.axis_size("kz"), lax.axis_size("tile")
     kz, tile = lax.axis_index("kz"), lax.axis_index("tile")
@@ -61,7 +61,6 @@
     lax.fori_loop(1, parts, greet_part, 0)
     pl.semaphore_wait(barrier, tiles + parts - 2)
     lax.fori_loop(1, parts, tell_part, 0)
-    pl.semaphore_wait(ready, parts - 1)
 
     def copy_to(part, spot, src, dst, send, recv):
         return pltpu.make_async_remote_copy(
@@ -91,6 +90,8 @@
 
     lax.fori_loop(0, devices, place, 0, unroll=8)
 
+    pl.semaphore_wait(ready, parts - 1)
+
     def send_met(k, carry):
         group = lax.rem(mine + k, groups)
         part, spot = group // columns, lax.rem(group, columns) * DEPTH + level
@@ -103,6 +104,7 @@
     own = pltpu.make_async_copy(data_ref.at[me], data_out.at[me], own_sem)
     own.start()
     met[mine] = spread[pl.ds(mine * DEPTH, DEPTH)]
+    basis_out[...] = basis_ref[...].astype(jnp.float32)
     others = pl.ds(0, groups - 1)
     rows = pl.ds(0, (groups - 1) * DEPTH)
     copy_to(kz, lax.rem(tile + 1, tiles), spread.at[rows], spread.at[rows], met_send, met_recv).wait_send()
@@ -120,6 +122,13 @@
 
     lax.fori_loop(1, DEPTH, send_frames, 0)
     frame_out[level] = total[level]
+
+    def clear(k, carry):
+        for h in range(2):
+            sums_out[h, k] = jnp.zeros(sums_out.shape[2:], jnp.float32)
+        return carry
+
+    lax.fori_loop(0, sums_out.shape[1], clear, 0)
     own.wait()
     others = pl.ds(0, devices - 1)
     levels = pl.ds(0, DEPTH - 1)
@@ -132,7 +141,7 @@
         every.wait_recv()
 
 
-def exchange(frames, data):
+def exchange(frames, basis, data):
     dma = pltpu.SemaphoreType.DMA
     devices = data.shape[0]
     groups = devices // DEPTH
@@ -141,19 +150,21 @@
         out_shape=[
             jax.ShapeDtypeStruct(data.shape, data.dtype),
             jax.ShapeDtypeStruct((DEPTH, 1, LANES), jnp.int32),
+            jax.ShapeDtypeStruct(basis.shape, jnp.float32),
+            jax.ShapeDtypeStruct((2, TILE_ROWS + 4, PAD, LANES), jnp.float32),
         ],
-        in_specs=[SMEM, HBM],
-        out_specs=[VMEM, VMEM],
+        in_specs=[SMEM, VMEM, HBM],
+        out_specs=[VMEM] * 4,
         scratch_shapes=[
             pltpu.VMEM((devices, 1, LANES), jnp.int32),
             pltpu.VMEM((groups, DEPTH, 1, LANES), jnp.int32),
             pltpu.VMEM((DEPTH, 1, LANES), jnp.int32),
             pltpu.SemaphoreType.REGULAR,
         ] + [dma] * 7,
-        compiler_params=pltpu.CompilerParams(collective_id=1, has_side_effects=True, vmem_limit_bytes=50 * MB),
-        cost_estimate=pl.CostEstimate(flops=0, bytes_accessed=4 * MB, transcendentals=0),
+        compiler_params=pltpu.CompilerParams(collective_id=1, has_side_effects=True, vmem_limit_bytes=8 * MB),
+        cost_estimate=pl.CostEstimate(flops=6 * 10**10, bytes_accessed=4 * MB, transcendentals=0),
         name="exchange",
-    )(frames, data)
+    )(frames, basis, data)
 
 
 def grid_slots(window_ref, live_ref, frame_ref, basis_ref, pos_ref, data_ref, acc_ref):
@@ -196,14 +207,8 @@
     lax.fori_loop(0, parts, step, 0)
 
 
-def grid_kernel(window_ref, live_ref, frame_ref, basis_ref, pos_ref, data_ref,
+def grid_kernel(window_ref, live_ref, frame_ref, basis_ref, pos_ref, data_ref, _,
                 inner_ref, own_ref, up_ref, down_ref, acc_ref):
-    def clear(k, carry):
-        for h in range(2):
-            acc_ref[h, k] = jnp.zeros(acc_ref.shape[2:], jnp.float32)
-        return carry
-
-    lax.fori_loop(0, acc_ref.shape[1], clear, 0)
     grid_slots(window_ref, live_ref, frame_ref, basis_ref, pos_ref, data_ref, acc_ref)
 
     def fold(row, carry):
@@ -240,7 +245,7 @@
     lax.fori_loop(0, TILE_ROWS - 4, emit, 0)
 
 
-def grid_tile(window, live, frames, basis, pos, data):
+def grid_tile(window, live, frames, basis, pos, data, sums):
     wide = 2 * LANES
     return pl.pallas_call(
         grid_kernel,
@@ -249,14 +254,15 @@
             jax.ShapeDtypeStruct((4, PLANE, wide), jnp.float32),
             jax.ShapeDtypeStruct((2, QUARTER, PLANE), jnp.bfloat16),
             jax.ShapeDtypeStruct((2, QUARTER, PLANE), jnp.bfloat16),
+            jax.ShapeDtypeStruct(sums.shape, sums.dtype),
         ],
-        in_specs=[SMEM] * 4 + [VMEM] * 2,
-        out_specs=[VMEM] * 4,
-        scratch_shapes=[pltpu.VMEM((2, TILE_ROWS + 4, PAD, LANES), jnp.float32)],
-        compiler_params=pltpu.CompilerParams(vmem_limit_bytes=40 * MB),
+        in_specs=[SMEM] * 4 + [VMEM] * 3,
+        out_specs=[VMEM] * 5,
+        input_output_aliases={6: 4},
+        compiler_params=pltpu.CompilerParams(vmem_limit_bytes=24 * MB),
         cost_estimate=pl.CostEstimate(flops=6 * 10**9, bytes_accessed=20 * MB, transcendentals=0),
         name="grid_tile",
-    )(window, live, frames, basis, pos, data)
+    )(window, live, frames, basis, pos, data, sums)[:4]
 
 
 def interleave(pieces):
@@ -501,11 +507,10 @@
     parts, tiles, slots, pair, samples = coil_data.shape[2:]
     devices = parts * tiles
     frames = frame_of[0, 0].transpose(0, 2, 1)
-    table = basis.T.astype(jnp.float32)
-    data, frames = exchange(frames, coil_data.reshape(devices, slots * pair, samples))
+    data, frames, table, sums = exchange(frames, basis.T, coil_data.reshape(devices, slots * pair, samples))
     window = window_at[0, 0].transpose(0, 2, 3, 1)
     pos = sample_pos.reshape(devices * slots, 2, samples)
-    inner, own, up, down = grid_tile(window, live_count[0, 0], frames, table, pos, data)
+    inner, own, up, down = grid_tile(window, live_count[0, 0], frames, table, pos, data, sums)
     ky_table, inner_table, edge_table = [jnp.asarray(t) for t in make_tables()]
     return transform_plane(ky_table, inner_table, edge_table, inner, own, up, down)[None]
 

time: 193 us -> 189 us (0.979)
  Pallas kernels: 186 us -> 182 us
    pallas_call x1, Pallas kernels: 60.6 us -> 56.7 us  [exchange(): pl.pallas_call(exchange_kernel, out_shape=[jax.ShapeDtypeStruct(data.shap...]
    unnamed x15 -> x19, local copies, waits for them, and re-layouts: 5.13 us -> 5.06 us
where the time goes in v7:
time: 189 us; the launch traced here: 187 us
  Pallas kernels  182 us (96%)
  local copies, waits for them, and re-layouts  5.06 us (3%)
    pallas_call x1, Pallas kernels, transform_plane(): pl.pallas_call(mid_kernel, out_shape=jax.ShapeDtypeStruct((PLANE, stages...  109 us
    pallas_call x1, Pallas kernels, exchange(): pl.pallas_call(exchange_kernel, out_shape=[jax.ShapeDtypeStruct(data.shap...  56.7 us
    pallas_call x1, Pallas kernels, grid_tile(): pl.pallas_call(grid_kernel, out_shape=[jax.ShapeDtypeStruct((TILE_ROWS -...  16.9 us
    unnamed x19, local copies, waits for them, and re-layouts  5.06 us

profile of v7, /device:TPU:32, one launch (start us, length us, event | category | flops | bytes accessed | tf_op | source)
XLA Modules:
  0.0 187.3 jit_solution(9616649614164784771)
XLA Ops:
  0.0 0.0 copy-start
  0.0 1.6 copy-done
  1.6 0.0 copy-start.2
  1.6 0.8 copy-done.2
  2.4 0.0 copy-start.4
  2.4 0.7 copy-done.4
  3.0 0.0 copy-start.1
  3.0 0.0 copy-start.3
  3.1 0.0 copy-start.5
  3.1 56.7 %exchange.1 = (bf16[256,32,128]{2,1,0:T(8,128)(2,1)S(1)}, s32[8,1,128]{2,1,0:T(1,128)S(1)}, f32[10,1000]{1,0:T(8,128)S(1)}, f32[2,24,672,128]{3,2,1,0:T(8,128)S(1)}) custom-call(s32[8,2,32]{2,1,0:T(2,128)S(1)} %bitcast.16, bf16[10,1000]{1,0:T(8,128)(2,1)S(1)} %bitcast.14, bf16[256,32,128]{2,1,0:T(8,128)(2,1)S(1)} %bitcast.12), custom_call_target="tpu_custom_call" | custom-call | flops 60000002048 | bytes 4194304 | tf_op jit(solution)/shard_map/exchange/pallas_call | solution.py:148
  59.8 0.0 copy-done.1
  59.8 0.0 copy-done.3
  59.8 0.0 copy-done.5
  59.8 0.0 copy-start.6
  59.9 0.0 copy-start.7
  59.9 0.0 copy-start.8
  59.9 16.9 %grid_tile.1 = (bf16[16,640,256]{2,1,0:T(8,128)(2,1)S(1)}, f32[4,640,256]{2,1,0:T(8,128)S(1)}, bf16[2,160,640]{2,1,0:T(8,128)(2,1)S(1)}, bf16[2,160,640]{2,1,0:T(8,128)(2,1)S(1)}, f32[2,24,672,128]{3,2,1,0:T(8,128)S(1)}) custom-call(s32[8,2,2,32]{3,2,1,0:T(2,128)S(1)} %bitcast.15, s32[8,32]{1,0:T(8,128)S(1)} %bitcast.17, ...), custom_call_target="tpu_custom_call", output_to_operand_aliasing={{4}: (6, {})} | custom-call | flops 6000000000 | bytes 20971520 | tf_op jit(solution)/shard_map/grid_tile/pallas_call | solution.py:250
  76.8 0.0 copy-done.6
  76.8 0.0 copy-done.7
  76.8 0.0 copy-done.8
  76.8 108.5 %plane.1 = bf16[640,3200]{1,0:T(8,128)(2,1)S(1)} custom-call(bf16[5,128,1280]{2,1,0:T(8,128)(2,1)S(1)} %copy-done.6, bf16[2,640,512]{2,1,0:T(8,128)(2,1)S(1)} %copy-done.7, bf16[2,640,128]{2,1,0:T(8,128)(2,1)S(1)} %copy-done.8, bf16[16,640,256]{2,1,0:T(8,128)(2,1)S(1)} %get-tuple-element.17.grid_ref, f32[4,640,256]{2,1,0:T(8,128)S(1)} %get-tuple-element.18.own_ref, ...), custom_call_target="tpu_custom_call" | custom-call | flops 20000000000 | bytes 20971520 | tf_op jit(solution)/shard_map/plane/pallas_call | solution.py:466
  185.3 2.0 %copy.13 = bf16[1,640,3200]{2,1,0:T(8,128)(2,1)} copy(bf16[1,640,3200]{2,1,0:T(8,128)(2,1)S(1)} %bitcast.11) | data formatting | bytes 8192000
Async XLA Ops:
  0.0 1.6 copy-start
  1.6 0.8 copy-start.2
  2.4 0.7 copy-start.4
  3.0 56.8 %copy-start.1 = (f32[1,1,8,32,2,2,128]{6,5,4,3,2,1,0:T(2,128)S(1)}, f32[1,1,8,32,2,2,128]{6,5,4,3,2,1,0:T(2,128)}, u32[]{:S(2)}) copy-start(f32[1,1,8,32,2,2,128]{6,5,4,3,2,1,0:T(2,128)} %param.12) | copy-start | bytes 1572868
  3.0 56.8 %copy-start.3 = (s32[1,1,8,32,2,2]{3,5,4,2,1,0:T(2,128)S(1)}, s32[1,1,8,32,2,2]{3,5,4,2,1,0:T(2,128)}, u32[]{:S(2)}) copy-start(s32[1,1,8,32,2,2]{3,5,4,2,1,0:T(2,128)} %param.13) | copy-start | bytes 12292
  3.1 56.8 %copy-start.5 = (s32[1,1,8,32]{3,2,1,0:T(8,128)S(1)}, s32[1,1,8,32]{3,2,1,0:T(8,128)}, u32[]{:S(2)}) copy-start(s32[1,1,8,32]{3,2,1,0:T(8,128)} %param.14) | copy-start | bytes 3076
  59.8 16.9 %copy-start.6 = (bf16[5,128,1280]{2,1,0:T(8,128)(2,1)S(1)}, bf16[5,128,1280]{2,1,0:T(8,128)(2,1)}, u32[]{:S(2)}) copy-start(bf16[5,128,1280]{2,1,0:T(8,128)(2,1)} %constant.6.clone.ky_ref) | copy-start | bytes 4915204
  59.9 16.9 %copy-start.7 = (bf16[2,640,512]{2,1,0:T(8,128)(2,1)S(1)}, bf16[2,640,512]{2,1,0:T(8,128)(2,1)}, u32[]{:S(2)}) copy-start(bf16[2,640,512]{2,1,0:T(8,128)(2,1)} %constant.7.clone.inner_table_ref) | copy-start | bytes 3932164
  59.9 16.9 %copy-start.8 = (bf16[2,640,128]{2,1,0:T(8,128)(2,1)S(1)}, bf16[2,640,128]{2,1,0:T(8,128)(2,1)}, u32[]{:S(2)}) copy-start(bf16[2,640,128]{2,1,0:T(8,128)(2,1)} %constant.8.clone.edge_table_ref) | copy-start | bytes 983044

commit v8 on v7

--- a/solution.py
+++ b/solution.py
@@ -291,7 +291,33 @@
     return pieces
 
 
-def mid_kernel(ky_ref, inner_table_ref, edge_table_ref, grid_ref, own_ref, up_ref, down_ref, out_ref,
+def joined(first, second):
+    lane = lax.rem(lax.broadcasted_iota(jnp.int32, first.shape, 1), 2 * HALF)
+    ahead = pltpu.roll(second, PLANE - HALF, 1)
+    behind = pltpu.roll(second, HALF, 1)
+    out = first + jnp.where(lane < HALF, -ahead, behind)
+    return (out * (1.0 / PLANE)).astype(jnp.bfloat16)
+
+
+def last_stage(edge_table_ref, before_ref, sums_ref, edge_ref, out_ref, block, sems):
+    done = before_ref.shape[1]
+    early = pltpu.make_async_copy(before_ref, out_ref.at[:, pl.ds(0, done)], sems.at[0])
+    early.start()
+    for h in range(2):
+        rows = slice(320 * h, 320 * (h + 1))
+        first, second = [
+            sums_ref[part, rows, :]
+            + jnp.dot(edge_table_ref[part, rows, :], edge_ref[...], preferred_element_type=jnp.float32)
+            for part in range(2)
+        ]
+        block[rows, :] = joined(first, second)
+    late = pltpu.make_async_copy(block, out_ref.at[:, pl.ds(done, PLANE)], sems.at[1])
+    late.start()
+    early.wait()
+    late.wait()
+
+
+def mid_kernel(ky_ref, inner_table_ref, edge_table_ref, grid_ref, own_ref, up_ref, down_ref, out_ref, last_ref, edge_ref,
                send_in, send_ed, recv_in, recv_ed, halo, rot, edge_grid, edge_rot, re_ref, im_ref, edge_kx,
                halo_send, halo_recv, send_sem_in, recv_sem_in, send_sem_ed, recv_sem_ed):
     count = lax.axis_size("tile")
@@ -410,9 +436,6 @@
 
     lax.fori_loop(0, stages, stage, 0)
 
-    lane = lax.rem(lax.broadcasted_iota(jnp.int32, (320, PLANE), 1), 2 * HALF)
-    real = lane < HALF
-
     def others(b, ref, send_sem, recv_sem):
         return pltpu.make_async_remote_copy(
             src_ref=ref.at[b, pl.ds(0, count - 1)], dst_ref=ref.at[b, pl.ds(0, count - 1)],
@@ -420,36 +443,43 @@
             device_id={"tile": below}, device_id_type=pl.DeviceIdType.MESH,
         )
 
-    def finish(b, carry):
-        others(b, recv_in, send_sem_in, recv_sem_in).wait_recv()
-        others(b, recv_ed, send_sem_ed, recv_sem_ed).wait_recv()
-
+    def lift_edges(b):
         def lift(s, carry):
             pair = [recv_ed[b, 2 * s + k].astype(jnp.float32) for k in range(2)]
             edge_kx[pl.ds(pl.multiple_of(8 * s, 8), 8), :] = jnp.concatenate(pair, axis=0)
             return carry
 
         lax.fori_loop(0, count // 2, lift, 0)
+        return edge_kx[...].astype(jnp.bfloat16)
+
+    def finish(b, carry):
+        others(b, recv_in, send_sem_in, recv_sem_in).wait_recv()
+        others(b, recv_ed, send_sem_ed, recv_sem_ed).wait_recv()
         inner = recv_in[b].reshape(count * inner_rows, PLANE)
-        edge = edge_kx[...].astype(jnp.bfloat16)
+        edge = lift_edges(b)
         for h in range(2):
             rows = slice(320 * h, 320 * (h + 1))
-
-            def product(part):
-                return jnp.dot(
-                    inner_table_ref[part, rows, :], inner, preferred_element_type=jnp.float32
-                ) + jnp.dot(edge_table_ref[part, rows, :], edge, preferred_element_type=jnp.float32)
-
-            first = product(0)
-            second = product(1)
-            ahead = pltpu.roll(second, PLANE - HALF, 1)
-            behind = pltpu.roll(second, HALF, 1)
-            out = first + jnp.where(real, -ahead, behind)
+            first, second = [
+                jnp.dot(inner_table_ref[part, rows, :], inner, preferred_element_type=jnp.float32)
+                + jnp.dot(edge_table_ref[part, rows, :], edge, preferred_element_type=jnp.float32)
+                for part in range(2)
+            ]
             at = pl.ds(pl.multiple_of(b * PLANE, PLANE), PLANE)
-            out_ref[rows, at] = (out * (1.0 / PLANE)).astype(jnp.bfloat16)
-        return carry
-
-    lax.fori_loop(0, stages, finish, 0)
+            out_ref[rows, at] = joined(first, second)
+        return carry
+
+    last = stages - 1
+    lax.fori_loop(0, last, finish, 0)
+    others(last, recv_in, send_sem_in, recv_sem_in).wait_recv()
+    inner = recv_in[last].reshape(count * inner_rows, PLANE)
+    for part in range(2):
+        for h in range(2):
+            rows = slice(320 * h, 320 * (h + 1))
+            last_ref[part, rows, :] = jnp.dot(
+                inner_table_ref[part, rows, :], inner, preferred_element_type=jnp.float32
+            )
+    others(last, recv_ed, send_sem_ed, recv_sem_ed).wait_recv()
+    edge_ref[...] = lift_edges(last)
 
     def sent(b, carry):
         others(b, send_in, send_sem_in, recv_sem_in).wait_send()
@@ -463,11 +493,15 @@
     stages, count, rows, wide = 5, 32, TILE_ROWS - 4, 2 * LANES
     bf16, f32 = jnp.bfloat16, jnp.float32
     dma = pltpu.SemaphoreType.DMA
-    return pl.pallas_call(
+    parts = pl.pallas_call(
         mid_kernel,
-        out_shape=jax.ShapeDtypeStruct((PLANE, stages * PLANE), bf16),
+        out_shape=[
+            jax.ShapeDtypeStruct((PLANE, (stages - 1) * PLANE), bf16),
+            jax.ShapeDtypeStruct((2, PLANE, PLANE), f32),
+            jax.ShapeDtypeStruct((4 * count, PLANE), bf16),
+        ],
         in_specs=[VMEM] * 7,
-        out_specs=VMEM,
+        out_specs=[VMEM] * 3,
         scratch_shapes=[
             pltpu.VMEM((stages, count, rows, PLANE), bf16),
             pltpu.VMEM((stages, count, 4, PLANE), bf16),
@@ -483,11 +517,21 @@
             dma((2,)), dma((2,)), dma((stages,)), dma((stages,)), dma((stages,)), dma((stages,)),
         ],
         compiler_params=pltpu.CompilerParams(
-            vmem_limit_bytes=36 * MB, collective_id=0, has_side_effects=True
+            vmem_limit_bytes=32 * MB, collective_id=0, has_side_effects=True
         ),
         cost_estimate=pl.CostEstimate(flops=20 * 10**9, bytes_accessed=20 * MB, transcendentals=0),
         name="plane",
     )(ky_table, inner_table, edge_table, grid, own, up, down)
+    return pl.pallas_call(
+        last_stage,
+        out_shape=jax.ShapeDtypeStruct((PLANE, stages * PLANE), bf16),
+        in_specs=[VMEM] * 4,
+        out_specs=HBM,
+        scratch_shapes=[pltpu.VMEM((PLANE, PLANE), bf16), dma((2,))],
+        compiler_params=pltpu.CompilerParams(vmem_limit_bytes=16 * MB),
+        cost_estimate=pl.CostEstimate(flops=5 * 10**8, bytes_accessed=8 * MB, transcendentals=0),
+        name="last_stage",
+    )(edge_table, *parts)
 
 
 def make_tables():

time: 189 us -> 187 us (0.989)
  local copies, waits for them, and re-layouts: 5.06 us -> 3.08 us
    unnamed x19 -> x18, local copies, waits for them, and re-layouts: 5.06 us -> 3.08 us
    pallas_call x1 -> x2, Pallas kernels: 109 us -> 109 us  [the longest x1 107 us: transform_plane(): pl.pallas_call(mid_kernel, out_shape=[jax.ShapeDtypeStruct((PLANE, (stage...]
where the time goes in v8:
time: 187 us; the launch traced here: 186 us
  Pallas kernels  183 us (98%)
  local copies, waits for them, and re-layouts  3.08 us (2%)
    pallas_call x1, Pallas kernels, transform_plane(): pl.pallas_call(mid_kernel, out_shape=[jax.ShapeDtypeStruct((PLANE, (stage...  107 us
    pallas_call x1, Pallas kernels, exchange(): pl.pallas_call(exchange_kernel, out_shape=[jax.ShapeDtypeStruct(data.shap...  56.7 us
    pallas_call x1, Pallas kernels, grid_tile(): pl.pallas_call(grid_kernel, out_shape=[jax.ShapeDtypeStruct((TILE_ROWS -...  16.7 us

profile of v8, /device:TPU:32, one launch (start us, length us, event | category | flops | bytes accessed | tf_op | source)
XLA Modules:
  0.0 186.1 jit_solution(16017632307214183224)
XLA Ops:
  0.0 0.0 copy-start.1
  0.0 1.6 copy-done.1
  1.6 0.0 copy-start.3
  1.6 0.8 copy-done.3
  2.4 0.0 copy-start.5
  2.4 0.7 copy-done.5
  3.0 0.0 copy-start.2
  3.0 0.0 copy-start.4
  3.1 0.0 copy-start.6
  3.1 56.7 %exchange.1 = (bf16[256,32,128]{2,1,0:T(8,128)(2,1)S(1)}, s32[8,1,128]{2,1,0:T(1,128)S(1)}, f32[10,1000]{1,0:T(8,128)S(1)}, f32[2,24,672,128]{3,2,1,0:T(8,128)S(1)}) custom-call(s32[8,2,32]{2,1,0:T(2,128)S(1)} %bitcast.15, bf16[10,1000]{1,0:T(8,128)(2,1)S(1)} %bitcast.13, bf16[256,32,128]{2,1,0:T(8,128)(2,1)S(1)} %bitcast.11), custom_call_target="tpu_custom_call" | custom-call | flops 60000002048 | bytes 4194304 | tf_op jit(solution)/shard_map/exchange/pallas_call | solution.py:148
  59.8 0.0 copy-done.2
  59.8 0.0 copy-done.4
  59.8 0.0 copy-done.6
  59.8 0.0 copy-start
  59.9 0.0 copy-start.7
  59.9 0.0 copy-start.8
  59.9 16.7 %grid_tile.1 = (bf16[16,640,256]{2,1,0:T(8,128)(2,1)S(1)}, f32[4,640,256]{2,1,0:T(8,128)S(1)}, bf16[2,160,640]{2,1,0:T(8,128)(2,1)S(1)}, bf16[2,160,640]{2,1,0:T(8,128)(2,1)S(1)}, f32[2,24,672,128]{3,2,1,0:T(8,128)S(1)}) custom-call(s32[8,2,2,32]{3,2,1,0:T(2,128)S(1)} %bitcast.14, s32[8,32]{1,0:T(8,128)S(1)} %bitcast.16, ...), custom_call_target="tpu_custom_call", output_to_operand_aliasing={{4}: (6, {})} | custom-call | flops 6000000000 | bytes 20971520 | tf_op jit(solution)/shard_map/grid_tile/pallas_call | solution.py:250
  76.6 0.0 copy-done
  76.6 0.0 copy-done.7
  76.6 0.0 copy-done.8
  76.6 107.0 %plane.1 = (bf16[640,2560]{1,0:T(8,128)(2,1)S(1)}, f32[2,640,640]{2,1,0:T(8,128)S(1)}, bf16[128,640]{1,0:T(8,128)(2,1)S(1)}) custom-call(bf16[5,128,1280]{2,1,0:T(8,128)(2,1)S(1)} %copy-done.7, bf16[2,640,512]{2,1,0:T(8,128)(2,1)S(1)} %copy-done.8, bf16[2,640,128]{2,1,0:T(8,128)(2,1)S(1)} %copy-done, bf16[16,640,256]{2,1,0:T(8,128)(2,1)S(1)} %get-tuple-element.20.grid_ref, ...), custom_call_target="tpu_custom_call" | custom-call | flops 20000000000 | bytes 20971520 | tf_op jit(solution)/shard_map/plane/pallas_call | solution.py:496
  183.6 2.4 %last_stage.1 = bf16[640,3200]{1,0:T(8,128)(2,1)} custom-call(bf16[2,640,128]{2,1,0:T(8,128)(2,1)S(1)} %copy-done, bf16[640,2560]{1,0:T(8,128)(2,1)S(1)} %get-tuple-element.24.before_ref, f32[2,640,640]{2,1,0:T(8,128)S(1)} %get-tuple-element.25.sums_ref, bf16[128,640]{1,0:T(8,128)(2,1)S(1)} %get-tuple-element.26.edge_ref), custom_call_target="tpu_custom_call" | custom-call | flops 500000000 | bytes 8388608 | tf_op jit(solution)/shard_map/last_stage/pallas_call | solution.py:525
Async XLA Ops:
  0.0 1.6 copy-start.1
  1.6 0.8 copy-start.3
  2.4 0.7 copy-start.5
  3.0 56.8 %copy-start.2 = (f32[1,1,8,32,2,2,128]{6,5,4,3,2,1,0:T(2,128)S(1)}, f32[1,1,8,32,2,2,128]{6,5,4,3,2,1,0:T(2,128)}, u32[]{:S(2)}) copy-start(f32[1,1,8,32,2,2,128]{6,5,4,3,2,1,0:T(2,128)} %param.12) | copy-start | bytes 1572868
  3.0 56.8 %copy-start.4 = (s32[1,1,8,32,2,2]{3,5,4,2,1,0:T(2,128)S(1)}, s32[1,1,8,32,2,2]{3,5,4,2,1,0:T(2,128)}, u32[]{:S(2)}) copy-start(s32[1,1,8,32,2,2]{3,5,4,2,1,0:T(2,128)} %param.13) | copy-start | bytes 12292
  3.1 56.8 %copy-start.6 = (s32[1,1,8,32]{3,2,1,0:T(8,128)S(1)}, s32[1,1,8,32]{3,2,1,0:T(8,128)}, u32[]{:S(2)}) copy-start(s32[1,1,8,32]{3,2,1,0:T(8,128)} %param.14) | copy-start | bytes 3076
  59.8 16.8 %copy-start = (bf16[2,640,128]{2,1,0:T(8,128)(2,1)S(1)}, bf16[2,640,128]{2,1,0:T(8,128)(2,1)}, u32[]{:S(2)}) copy-start(bf16[2,640,128]{2,1,0:T(8,128)(2,1)} %constant.8.clone.edge_table_ref) | copy-start | bytes 983044
  59.9 16.8 %copy-start.7 = (bf16[5,128,1280]{2,1,0:T(8,128)(2,1)S(1)}, bf16[5,128,1280]{2,1,0:T(8,128)(2,1)}, u32[]{:S(2)}) copy-start(bf16[5,128,1280]{2,1,0:T(8,128)(2,1)} %constant.6.clone.ky_ref) | copy-start | bytes 4915204
  59.9 16.8 %copy-start.8 = (bf16[2,640,512]{2,1,0:T(8,128)(2,1)S(1)}, bf16[2,640,512]{2,1,0:T(8,128)(2,1)}, u32[]{:S(2)}) copy-start(bf16[2,640,512]{2,1,0:T(8,128)(2,1)} %constant.7.clone.inner_table_ref) | copy-start | bytes 3932164
